TPU v7x, 512 devices: a whole 4x4x16 slice. The times are simulated.
512 devices in a mesh: row: 16 (over z), col: 8 (over x, core), rep: 4 (over y).
Axes of the slice: x: 4, y: 4, z: 16, core: 2. Of those that a mesh axis runs over, the one named last changes fastest.
Arguments:
- density: bfloat16 [6144, 6144], P('row', 'col'), as said below
- keep_square: int32 [48, 48], P('row', 'col'), may hold values 0 or 1
- keep_cube: int32 [48, 48], P('row', 'col'), may hold values 0 or 1
Outputs:
- purified: float32 [6144, 6144], P(('row', 'rep'), 'col')
Inputs may be any that keep to these rules, and one draw needn't show every extreme that they name: density is symmetric; its 128 x 128 diagonal blocks are always occupied, any other block may be zero or occupied at any distance from the diagonal.
All inputs are finite; a program needn't handle non-finite values. No bound on the sum of `keep_square` or of `keep_cube` on one device may be relied on, other than what follows from the above.
Results may differ from a plain program's by a relative error of at most 0.002.
Values may be sent and summed in bfloat16 or wider, within the bound.
No kernel may reach another device: no remote copies, remote signals or barrier semaphores. Data moves between devices by JAX's collectives and lax.ppermute only.
A program may use at most 64 MiB of HBM per device.

v0:
```python
import jax
import jax.numpy as jnp
from jax import lax
from jax.sharding import PartitionSpec as P

BLK = 128


def broadcast(array, axis, root):
    mine = lax.axis_index(axis) == root
    return lax.psum(jnp.where(mine, array, jnp.zeros_like(array)), axis)


def widen(mask, tile_rows, tile_cols):
    blocks = jnp.broadcast_to(
        mask.astype(jnp.float32)[:, None, :, None], (mask.shape[0], BLK, mask.shape[1], BLK)
    )
    return blocks.reshape(tile_rows, tile_cols)


def left_piece(tile, piece_index):
    height = tile.shape[0]
    per_tile = tile.shape[1] // height
    column = lax.dynamic_slice_in_dim(tile, piece_index % per_tile * height, height, 1)
    return broadcast(column, "col", piece_index // per_tile)


def right_piece(density, piece_index):
    return broadcast(density, "row", piece_index)


def local(density, keep_square, keep_cube):
    tile_rows, tile_cols = density.shape
    rep_count = lax.axis_size("rep")
    row_count = lax.axis_size("row")
    rep_index = lax.axis_index("rep")
    sections = row_count // rep_count
    indices = [position * rep_count + rep_index for position in range(sections)]
    square_total = jnp.zeros((tile_rows, tile_cols), jnp.float32)
    for piece_index in indices:
        right_panel = right_piece(density, piece_index)
        square_total = square_total + jnp.dot(
            left_piece(density, piece_index), right_panel, preferred_element_type=jnp.float32
        )
    square_total = square_total * widen(keep_square, tile_rows, tile_cols)
    square_own = lax.psum_scatter(square_total, "rep", scatter_dimension=0, tiled=True)
    square_low = lax.all_gather(square_own.astype(jnp.bfloat16), "rep", axis=0, tiled=True)
    cube_total = jnp.zeros((tile_rows, tile_cols), jnp.float32)
    for number, piece_index in enumerate(indices):
        right_panel = right_piece(density, piece_index)
        cube_total = cube_total + jnp.dot(
            left_piece(square_low, piece_index), right_panel, preferred_element_type=jnp.float32
        )
    cube_total = cube_total * widen(keep_cube, tile_rows, tile_cols)
    cube_own = lax.psum_scatter(cube_total, "rep", scatter_dimension=0, tiled=True)
    return 3.0 * square_own - 2.0 * cube_own


def solution(mesh):
    return jax.shard_map(
        local,
        mesh=mesh,
        in_specs=(P("row", "col"), P("row", "col"), P("row", "col")),
        out_specs=P(("row", "rep"), "col"),
        check_vma=False,
    )
```

profile of v0, /device:TPU:1, one launch (start us, length us, event | category | flops | bytes accessed | tf_op | source)
XLA Modules:
  0.0 414.0 jit_solution(2673352959636272408)
XLA Ops:
  6.5 2.5 dynamic-slice_select_fusion.4
  9.2 1.0 copy-done
  10.1 1.5 broadcast_select_fusion
  11.7 0.6 copy-done.12
  12.3 79.8 %all-reduce.11.cloned.1.call-done = (bf16[384,384]{1,0:T(8,128)(2,1)}, bf16[384,384]{1,0:T(8,128)(2,1)}, bf16[384,384]{1,0:T(8,128)(2,1)}, bf16[384,384]{1,0:T(8,128)(2,1)}) async-done(((bf16[384,384]{1,0:T(8,128)(2,1)}, bf16[384,384]{1,0:T(8,128)(2,1)}, bf16[384,384]{1,0:T(8,128)(2,1)}, bf16[384,384]{1,0:T(8,128)(2,1)}), (bf16[384,384]{1,0:T(8,128)(2,1)}, bf16[384,384]{1,0:T(8,128)(2,1)}, ...) | async-done | bytes 1179664 | tf_op jit(solution)/shard_map/psum | solution.py:11
  92.2 141.3 %all-reduce.7.cloned.1.call-done = (bf16[384,768]{1,0:T(8,128)(2,1)}, bf16[384,768]{1,0:T(8,128)(2,1)}, bf16[384,768]{1,0:T(8,128)(2,1)}, bf16[384,768]{1,0:T(8,128)(2,1)}) async-done(((bf16[384,768]{1,0:T(8,128)(2,1)}, bf16[384,768]{1,0:T(8,128)(2,1)}, bf16[384,768]{1,0:T(8,128)(2,1)}, bf16[384,768]{1,0:T(8,128)(2,1)}), (bf16[384,768]{1,0:T(8,128)(2,1)}, bf16[384,768]{1,0:T(8,128)(2,1)}, ...) | async-done | bytes 2359312 | tf_op jit(solution)/shard_map/psum | solution.py:11
  233.4 1.7 fusion.2
  235.1 0.5 convolution_add_fusion.5
  235.6 0.6 copy-done.2
  236.2 0.1 copy-done.7
  236.3 0.5 convolution_add_fusion.4
  236.7 0.2 broadcast_in_dim.4
  236.9 0.9 copy-done.1
  237.8 0.1 copy-done.6
  237.9 1.5 fusion
  239.4 0.0 all-reduce.9.cloned.1.call-start
  239.5 35.5 %reduce-scatter.3.cloned.1.call-done = f32[96,768]{1,0:T(8,128)} async-done(((f32[384,768]{1,0:T(8,128)}), f32[96,768]{1,0:T(8,128)}) %reduce-scatter.3.cloned.1.call-update) | async-done | bytes 294928 | tf_op jit(solution)/shard_map/reduce_scatter | solution.py:46
  275.0 1.0 convert_element_type.10
  276.0 11.0 %all_gather.3 = bf16[384,768]{1,0:T(8,128)(2,1)S(1)} all-gather(bf16[96,768]{1,0:T(8,128)(2,1)S(1)} %convert_element_type.10), channel_id=1, replica_groups=mesh['row'=16,'col'=8,'rep'=4] {'rep'}, dimensions={0}, use_global_device_ids=true | all-gather | bytes 737280 | tf_op jit(solution)/shard_map/all_gather | solution.py:47
  286.9 1.1 dynamic-slice_select_fusion
  288.1 0.0 reduce-scatter.5.cloned.1.call-start
  288.1 0.6 copy-done.13
  288.7 79.7 %all-reduce.9.cloned.1.call-done = (bf16[384,384]{1,0:T(8,128)(2,1)}, bf16[384,384]{1,0:T(8,128)(2,1)}, bf16[384,384]{1,0:T(8,128)(2,1)}, bf16[384,384]{1,0:T(8,128)(2,1)}) async-done(((bf16[384,384]{1,0:T(8,128)(2,1)}, bf16[384,384]{1,0:T(8,128)(2,1)}, bf16[384,384]{1,0:T(8,128)(2,1)}, bf16[384,384]{1,0:T(8,128)(2,1)}), (bf16[384,384]{1,0:T(8,128)(2,1)}, bf16[384,384]{1,0:T(8,128)(2,1)}, ...) | async-done | bytes 1179664 | tf_op jit(solution)/shard_map/psum | solution.py:11
  368.5 1.5 fusion.3
  370.0 0.5 convolution_add_fusion.2
  370.4 0.5 copy-done.10
  370.9 0.5 convolution_add_fusion.1
  371.4 0.2 broadcast_in_dim.5
  371.6 0.8 copy-done.9
  372.4 1.5 fusion.1
  373.9 31.8 %reduce-scatter.5.cloned.1.call-done = f32[96,768]{1,0:T(8,128)} async-done(((f32[384,768]{1,0:T(8,128)}), f32[96,768]{1,0:T(8,128)}) %reduce-scatter.5.cloned.1.call-update) | async-done | bytes 294928 | tf_op jit(solution)/shard_map/reduce_scatter | solution.py:55
  405.7 1.7 multiply_subtract_fusion
  (29 shorter events, 0.2 us)
Async XLA Ops:
  6.5 85.6 %all-reduce.11.cloned.1.call-start = ((), (), s32[]{:S(2)}) async-start(), calls=%async_computation.6 | async-start | bytes 2359296 | tf_op jit(solution)/shard_map/psum | solution.py:11
  9.1 1.1 copy-start
  9.1 224.3 %all-reduce.7.cloned.1.call-start = ((), (), s32[]{:S(2)}) async-start(), calls=%async_computation.4 | async-start | bytes 4718592 | tf_op jit(solution)/shard_map/psum | solution.py:11
  11.6 0.7 copy-start.12
  11.7 263.3 %reduce-scatter.3.cloned.1.call-start = ((), (), s32[]{:S(2)}) async-start(), calls=%async_computation.2 | async-start | bytes 1474560 | tf_op jit(solution)/shard_map/reduce_scatter | solution.py:46
  92.1 142.9 %copy-start.8 = (bf16[384,384]{1,0:T(8,128)(2,1)S(1)}, bf16[384,384]{1,0:T(8,128)(2,1)}, u32[]{:S(2)}) copy-start(bf16[384,384]{1,0:T(8,128)(2,1)} %get-tuple-element.14) | copy-start | bytes 884740
  233.4 1.7 copy-start.3
  235.1 1.1 copy-start.2
  235.1 1.1 copy-start.7
  236.7 1.1 copy-start.1
  236.7 1.1 copy-start.6
  239.4 129.1 %all-reduce.9.cloned.1.call-start = ((), (), s32[]{:S(2)}) async-start(), calls=%async_computation.5 | async-start | bytes 2359296 | tf_op jit(solution)/shard_map/psum | solution.py:11
  288.0 0.7 copy-start.13
  288.0 80.4 %copy-start.4 = (bf16[384,768]{1,0:T(8,128)(2,1)S(1)}, bf16[384,768]{1,0:T(8,128)(2,1)}, u32[]{:S(2)}) copy-start(bf16[384,768]{1,0:T(8,128)(2,1)} %get-tuple-element.5) | copy-start | bytes 1769476
  288.1 117.6 %reduce-scatter.5.cloned.1.call-start = ((), (), s32[]{:S(2)}) async-start(), calls=%async_computation.3 | async-start | bytes 1474560 | tf_op jit(solution)/shard_map/reduce_scatter | solution.py:55
  368.5 1.5 copy-start.11
  370.0 1.0 copy-start.10
  371.4 1.0 copy-start.9
  373.9 31.8 %copy-start.5 = (f32[96,768]{1,0:T(8,128)S(1)}, f32[96,768]{1,0:T(8,128)}, u32[]{:S(2)}) copy-start(f32[96,768]{1,0:T(8,128)} %reduce-scatter.3.cloned.1.call-done) | copy-start | bytes 884740
Sparse Core Ops, SparseCore 0:
  9.9 82.1 all-reduce.10
  94.7 138.6 all-reduce.6
  239.5 35.3 reduce-scatter.2
  288.2 80.2 all-reduce.8
  374.0 31.6 reduce-scatter.4
where the time goes:
time: 415 us; the launch traced here: 414 us
  waiting for transfers between devices  368 us (89%)
  between operations  13.3 us (3%)
  blocking collectives  11 us (3%)
  matrix products  8.08 us (2%)
  other arithmetic  7.85 us (2%)
  local copies, waits for them, and re-layouts  5.4 us (1%)
    psum x3, waiting for transfers between devices, broadcast(): return lax.psum(jnp.where(mine, array, jnp.zeros_like(array)), axis)  301 us
    reduce_scatter x1, waiting for transfers between devices, local(): lax.psum_scatter(square_total, 'rep', scatter_dimension=0, tiled=True)  35.5 us
    reduce_scatter x1, waiting for transfers between devices, local(): lax.psum_scatter(cube_total, 'rep', scatter_dimension=0, tiled=True)  31.8 us
    all_gather x1, blocking collectives, local(): lax.all_gather(square_own.astype(jnp.bfloat16), 'rep', axis=0, tiled=True)  11 us
  transfers between devices with their start and end apart: 5, of which 5 were waited for; matrix products, arithmetic and copies ran while one was open for 0% of the time, Pallas kernels for 0%

commit v1 on v0

v1 whole, which is shorter than its diff:
```python
import jax
import jax.numpy as jnp
from jax import lax
from jax.sharding import PartitionSpec as P

BLK = 128
TOP = 16384.0
TINY = 1.1754943508222875e-38
PAD = 16


def encode(piece):
    values = piece.astype(jnp.float32)
    largest = jnp.max(jnp.abs(values), axis=0, keepdims=True)
    exponent = jnp.floor(jnp.log2(jnp.maximum(largest, TINY)))
    coded = (values * jnp.exp2(-exponent) * TOP).astype(jnp.float16)
    header = jnp.broadcast_to(exponent, (PAD, piece.shape[1])).astype(jnp.float16)
    return jnp.concatenate([coded, header], axis=0)


def decode(coded, count):
    parts = coded.reshape(count, -1, coded.shape[1]).astype(jnp.float32)
    height = parts.shape[1] - PAD
    scale = jnp.exp2(parts[:, height : height + 1, :])
    values = (parts[:, :height, :] * (1.0 / TOP) * scale).astype(jnp.bfloat16)
    return values.reshape(count * height, coded.shape[1])


def local(density, keep_square, keep_cube):
    tile_rows, tile_cols = density.shape
    reps = lax.axis_size("rep")
    row_count = lax.axis_size("row")
    col_count = lax.axis_size("col")
    rep = lax.axis_index("rep")
    own = tile_rows // reps
    halves = tile_cols // tile_rows

    def section(array):
        cut = [
            lax.dynamic_slice_in_dim(array, half * tile_rows + rep * own, own, 0)
            for half in range(halves)
        ]
        return jnp.concatenate(cut, axis=0)

    right_piece = lax.dynamic_slice_in_dim(density, rep * own, own, 0)
    left_piece = section(density.T)
    left = decode(lax.all_gather(encode(left_piece), "col", axis=0, tiled=True), col_count)
    right = decode(lax.all_gather(encode(right_piece), "row", axis=0, tiled=True), row_count)

    def contract(a, b):
        return lax.dot_general(a, b, (((0,), (0,)), ((), ())), preferred_element_type=jnp.float32)

    partial = contract(right, left)
    partial = partial.reshape(halves, reps, own, tile_rows).transpose(1, 0, 2, 3)
    partial = partial.reshape(reps, halves * own, tile_rows)
    square_t = jnp.sum(lax.all_to_all(partial, "rep", 0, 0), axis=0)
    mask_rows = section(jnp.repeat(keep_square.T.astype(jnp.float32), BLK, axis=0))
    square_t = square_t * jnp.repeat(mask_rows, BLK, axis=1)

    low = decode(
        lax.all_gather(encode(square_t.astype(jnp.bfloat16)), "col", axis=0, tiled=True), col_count
    )
    cube = contract(low, right)
    mask = jnp.repeat(jnp.repeat(keep_cube.astype(jnp.float32), BLK, axis=0), BLK, axis=1)
    placed = jnp.zeros((tile_cols, tile_rows), jnp.float32)
    for half in range(halves):
        placed = lax.dynamic_update_slice_in_dim(
            placed, square_t[half * own : (half + 1) * own], half * tile_rows + rep * own, 0
        )
    total = 3.0 * placed.T - 2.0 * cube * mask
    pieces = lax.all_to_all(total.reshape(reps, own, tile_cols), "rep", 0, 0)
    return jnp.sum(pieces, axis=0)


def solution(mesh):
    return jax.shard_map(
        local,
        mesh=mesh,
        in_specs=(P("row", "col"), P("row", "col"), P("row", "col")),
        out_specs=P(("row", "rep"), "col"),
        check_vma=False,
    )
```

time: 415 us -> 157 us (0.38)
  waiting for transfers between devices: 368 us -> 13.1 us
  blocking collectives: 11 us -> 105 us
  local copies, waits for them, and re-layouts: 5.4 us -> 19.1 us
  between operations: 13.3 us -> 0.22 us
  starting transfers between devices: 0.17 us -> 4.39 us
    psum x3 -> x0, waiting for transfers between devices: 301 us -> none  [broadcast(): return lax.psum(jnp.where(mine, array, jnp.zeros_like(array)), axis)]
    all_gather x1 -> x3, blocking collectives: 11 us -> 86.6 us  [the longest x1 49.8 us: local(): lax.all_gather(encode(right_piece), 'row', axis=0, tiled=True)]
    reduce_scatter x2 -> x0, waiting for transfers between devices: 67.3 us -> none  [the longest x1 35.5 us: local(): lax.psum_scatter(square_total, 'rep', scatter_dimension=0, tiled=True)]
    all_to_all x0 -> x1, blocking collectives: none -> 18.7 us  [local(): pieces = lax.all_to_all(total.reshape(reps, own, tile_cols), 'rep', 0, 0)]
    all_to_all x0 -> x1, waiting for transfers between devices: none -> 13.1 us  [local(): square_t = jnp.sum(lax.all_to_all(partial, 'rep', 0, 0), axis=0)]
    select_n x3 -> x0, other arithmetic: 5.15 us -> none  [broadcast(): return lax.psum(jnp.where(mine, array, jnp.zeros_like(array)), axis)]
    all_to_all x0 -> x1, starting transfers between devices: none -> 4.39 us  [local(): square_t = jnp.sum(lax.all_to_all(partial, 'rep', 0, 0), axis=0)]
  transfers between devices with their start and end apart: 5 -> 1, of which waited for: 5 -> 1; matrix products, arithmetic and copies ran while one was open for 0% -> 2% of each run, Pallas kernels for 0% -> 0%
where the time goes in v1:
time: 157 us
  blocking collectives  105 us (67%)
  local copies, waits for them, and re-layouts  19.1 us (12%)
  waiting for transfers between devices  13.1 us (8%)
  other arithmetic  10.5 us (7%)
  starting transfers between devices  4.39 us (3%)
  matrix products  4.17 us (3%)
    all_gather x1, blocking collectives, local(): lax.all_gather(encode(right_piece), 'row', axis=0, tiled=True)  49.8 us
    all_gather x1, blocking collectives, local(): lax.all_gather(encode(left_piece), 'col', axis=0, tiled=True)  21.3 us
    all_to_all x1, blocking collectives, local(): pieces = lax.all_to_all(total.reshape(reps, own, tile_cols), 'rep', 0, 0)  18.7 us
    all_gather x1, blocking collectives, local(): lax.all_gather(encode(square_t.astype(jnp.bfloat16)), 'col', axis=0, tile...  15.4 us
    all_to_all x1, waiting for transfers between devices, local(): square_t = jnp.sum(lax.all_to_all(partial, 'rep', 0, 0), axis=0)  13.1 us
    all_to_all x1, starting transfers between devices, local(): square_t = jnp.sum(lax.all_to_all(partial, 'rep', 0, 0), axis=0)  4.39 us
    dot_general x2, matrix products, contract(): lax.dot_general(a, b, (((0,), (0,)), ((), ())), preferred_element_type=jn...  4.17 us
    dynamic_update_slice x2, local copies, waits for them, and re-layouts, local(): lax.dynamic_update_slice_in_dim(placed, square_t[half * own:(half + 1) *...  3.9 us
  transfers between devices with their start and end apart: 1, of which 1 were waited for; matrix products, arithmetic and copies ran while one was open for 2% of the time, Pallas kernels for 0%

profile of v1, /device:TPU:1, one launch (start us, length us, event | category | flops | bytes accessed | tf_op | source)
XLA Modules:
  0.0 156.7 jit_solution(12126970050853005048)
XLA Ops:
  0.0 0.9 fusion.11
  1.0 1.0 fusion.13
  2.0 49.8 %all-gather.3 = f16[1792,768]{1,0:T(8,128)(2,1)S(1)} all-gather(f16[112,768]{1,0:T(8,128)(2,1)S(1)} %pad_maximum_fusion.3), channel_id=1, replica_groups=mesh['row'=16,'col'=8,'rep'=4] {'row'}, dimensions={0}, use_global_device_ids=true | all-gather | bytes 2924544 | tf_op jit(solution)/shard_map/all_gather | solution.py:48
  51.8 0.5 convert.3
  52.5 0.5 fusion
  53.0 2.4 %copy.12 = bf16[1536,768]{0,1:T(8,128)(2,1)} copy(bf16[1536,768]{1,0:T(8,128)(2,1)S(1)} %bitcast.59) | data formatting | bytes 4718592 | tf_op jit(solution)/shard_map/reshape | solution.py:26
  55.5 1.1 dynamic-slice_bitcast_fusion.1
  56.6 0.2 fusion.5
  57.3 0.2 copy.13
  57.5 21.3 %all-gather.4 = f16[1664,384]{1,0:T(8,128)(2,1)S(1)} all-gather(f16[208,384]{1,0:T(8,128)(2,1)S(1)} %copy.13), channel_id=1, replica_groups=mesh['row'=16,'col'=8,'rep'=4] {'col'}, dimensions={0}, use_global_device_ids=true | all-gather | bytes 1437696 | tf_op jit(solution)/shard_map/all_gather | solution.py:47
  79.1 0.2 fusion.2
  79.3 1.4 copy-done
  80.7 1.4 convolution_bitcast_fusion
  82.1 1.1 copy.14
  83.3 4.4 %all-to-all-start = ((f32[4,192,384]{2,1,0:T(8,128)}), f32[4,192,384]{2,1,0:T(8,128)}, u32[]{:S(2)}, u32[]{:S(2)}) async-start(f32[4,192,384]{2,1,0:T(8,128)} %bitcast.13), calls=%async_computation | async-start | bytes 2359296 | tf_op jit(solution)/shard_map/all_to_all | solution.py:56
  87.9 1.1 broadcast_in_dim.40
  89.0 1.6 %copy.18 = f32[384,768]{1,0:T(8,128)S(1)} copy(f32[384,768]{0,1:T(8,128)} %bitcast.66) | data formatting | bytes 2359296 | tf_op jit(solution)/shard_map/reshape | solution.py:64
  90.8 13.1 %all-to-all-done = f32[4,192,384]{2,1,0:T(8,128)} async-done(((f32[4,192,384]{2,1,0:T(8,128)}), f32[4,192,384]{2,1,0:T(8,128)}, u32[]{:S(2)}, u32[]{:S(2)}) %all-to-all-start) | async-done | bytes 1179680 | tf_op jit(solution)/shard_map/all_to_all | solution.py:56
  103.9 2.1 %reduce_sum.18 = f32[192,384]{1,0:T(8,128)} reduce(f32[4,192,384]{2,1,0:T(8,128)} %all-to-all-done, f32[]{:T(128)} %constant.15.clone.1), dimensions={0}, to_apply=%region_2.0 | reduce | flops 221184 | bytes 1474564 | tf_op jit(solution)/shard_map/reduce_sum | solution.py:56
  106.0 1.9 %copy.15 = f32[192,384]{0,1:T(8,128)} copy(f32[192,384]{1,0:T(8,128)} %reduce_sum.18) | data formatting | bytes 589824 | tf_op jit(solution)/shard_map/reduce_sum | solution.py:56
  107.9 1.1 fusion.8
  109.0 0.8 fusion.23
  110.1 0.8 pad_maximum_fusion.2
  110.9 1.7 %copy.16 = f16[208,384]{1,0:T(8,128)(2,1)} copy(f16[208,384]{0,1:T(8,128)(2,1)} %pad_maximum_fusion.2) | data formatting | bytes 319488 | tf_op jit(solution)/shard_map/concatenate | solution.py:18
  112.6 15.4 %all-gather.5 = f16[1664,384]{1,0:T(8,128)(2,1)S(1)} all-gather(f16[208,384]{1,0:T(8,128)(2,1)} %copy.16), channel_id=1, replica_groups=mesh['row'=16,'col'=8,'rep'=4] {'col'}, dimensions={0}, use_global_device_ids=true | all-gather | bytes 1437696 | tf_op jit(solution)/shard_map/all_gather | solution.py:61
  128.2 1.2 fusion.1
  129.4 1.1 broadcast_in_dim.16
  130.6 2.0 %dynamic_update_slice.6 = f32[768,384]{0,1:T(8,128)} dynamic-update-slice(f32[768,384]{0,1:T(8,128)} %broadcast_in_dim.16, f32[96,384]{0,1:T(8,128)} %get-tuple-element.10, s32[]{:T(128)S(6)} %select_n.14, s32[]{:T(128)} %constant.18.clone.1) | dynamic-update-slice | bytes 294916 | tf_op jit(solution)/shard_map/dynamic_update_slice | solution.py:67
  132.5 1.9 %dynamic_update_slice.7 = f32[768,384]{0,1:T(8,128)} dynamic-update-slice(f32[768,384]{0,1:T(8,128)} %dynamic_update_slice.6, f32[96,384]{0,1:T(8,128)} %get-tuple-element.9, s32[]{:T(128)S(6)} %select_n.15, s32[]{:T(128)} %constant.18.clone.1) | dynamic-update-slice | bytes 294916 | tf_op jit(solution)/shard_map/dynamic_update_slice | solution.py:67
  134.5 2.8 %fusion.4 = f32[384,768]{1,0:T(8,128)S(1)} fusion(f32[384,768]{1,0:T(8,128)S(1)} %copy.18, bf16[1536,384]{1,0:T(8,128)(2,1)} %bitcast.65, bf16[1536,768]{1,0:T(8,128)(2,1)S(1)} %bitcast.60, f32[768,384]{0,1:T(8,128)} %dynamic_update_slice.7), kind=kOutput, calls=%fused_computation.9 | convolution fusion | flops 907149312 | bytes 7077888 | tf_op jit(solution)/shard_map/dot_general | solution.py:51
  137.3 18.7 %all_to_all.10 = f32[4,96,768]{2,1,0:T(8,128)S(1)} all-to-all(f32[4,96,768]{2,1,0:T(8,128)S(1)} %bitcast.64), channel_id=1, replica_groups=mesh['row'=16,'col'=8,'rep'=4] {'rep'}, dimensions={0} | all-to-all | bytes 2359296 | tf_op jit(solution)/shard_map/all_to_all | solution.py:71
  155.9 0.8 reduce_sum.19
  (32 shorter events, 1.7 us)
Async XLA Ops:
  79.1 1.7 %copy-start = (bf16[1536,768]{0,1:T(8,128)(2,1)S(1)}, bf16[1536,768]{0,1:T(8,128)(2,1)}, u32[]{:S(2)}) copy-start(bf16[1536,768]{0,1:T(8,128)(2,1)} %copy.12) | copy-start | bytes 7077892
  83.2 4.4 %copy-start.1 = (s32[3,6]{1,0:T(4,128)S(1)}, s32[3,6]{1,0:T(4,128)}, u32[]{:S(2)}) copy-start(s32[3,6]{1,0:T(4,128)} %param.4) | copy-start | bytes 220
  83.2 4.5 %copy-start.2 = (s32[3,6]{1,0:T(4,128)S(1)}, s32[3,6]{1,0:T(4,128)}, u32[]{:S(2)}) copy-start(s32[3,6]{1,0:T(4,128)} %param.5) | copy-start | bytes 220
  83.3 20.7 %all-to-all-start = ((f32[4,192,384]{2,1,0:T(8,128)}), f32[4,192,384]{2,1,0:T(8,128)}, u32[]{:S(2)}, u32[]{:S(2)}) async-start(f32[4,192,384]{2,1,0:T(8,128)} %bitcast.13), calls=%async_computation | async-start | bytes 2359296 | tf_op jit(solution)/shard_map/all_to_all | solution.py:56

commit v2 on v0

v2 whole, which is shorter than its diff:
```python
import functools

import jax
import jax.numpy as jnp
from jax import lax
from jax.experimental import pallas as pl
from jax.experimental.pallas import tpu as pltpu
from jax.sharding import PartitionSpec as P

BLK = 128
TOP = 8192.0
LOWEST, HIGHEST = -100.0, 126.0
HEAD = 8

SMEM = pl.BlockSpec(memory_space=pltpu.SMEM)
VMEM = pl.BlockSpec(memory_space=pltpu.VMEM)


def call(kernel, out_shape, in_specs, scratch=()):
    return pl.pallas_call(
        kernel,
        out_shape=out_shape,
        in_specs=in_specs,
        scratch_shapes=list(scratch),
        compiler_params=pltpu.CompilerParams(vmem_limit_bytes=48 << 20),
    )


def contract(a, b):
    return lax.dot_general(a, b, (((0,), (0,)), ((), ())), preferred_element_type=jnp.float32)


def scaled(values):
    largest = jnp.max(jnp.abs(values), axis=0, keepdims=True)
    exponent = jnp.floor(jnp.log2(jnp.maximum(largest, 2.0**LOWEST)))
    exponent = jnp.clip(exponent, LOWEST, HIGHEST)
    return values * jnp.exp2(-exponent) * TOP, exponent


def store_coded(ref, values):
    coded, exponent = scaled(values)
    height = values.shape[0]
    ref[:height, :] = coded.astype(jnp.bfloat16)
    ref[height:, :] = jnp.broadcast_to(exponent, (ref.shape[0] - height, values.shape[1])).astype(
        jnp.bfloat16
    )


def gather(coded, axis):
    whole = lax.all_gather(coded.astype(jnp.float16), axis)
    count, height, width = whole.shape
    height -= HEAD
    scale = jnp.exp2(whole[:, height : height + 1, :].astype(jnp.float32))
    values = whole[:, :height, :].astype(jnp.float32) * (1.0 / TOP) * scale
    return values.astype(jnp.bfloat16).reshape(count * height, width)


def prepare(own, halves, rep_ref, tile_ref, right_ref, left_ref, turned):
    rows = tile_ref.shape[0]
    start = pl.multiple_of(rep_ref[0] * own, own)
    store_coded(right_ref, tile_ref[pl.ds(start, own), :].astype(jnp.float32))
    turned[...] = tile_ref[...].T
    for half in range(halves):
        piece = turned[pl.ds(pl.multiple_of(half * rows + start, own), own), :]
        for to in range(left_ref.shape[0]):
            left_ref[to, half * own : (half + 1) * own, :] = piece


def square_part(own, halves, right_ref, left_ref, out_ref):
    product = contract(right_ref[...], left_ref[...])
    rows = product.shape[0] // halves
    for rep in range(out_ref.shape[0]):
        for half in range(halves):
            first = half * rows + rep * own
            out_ref[rep, half * own : (half + 1) * own, :] = product[first : first + own, :]


def square_sum(own, halves, rep_ref, keep_ref, parts_ref, square_ref, low_ref):
    total = parts_ref[0]
    for rep in range(1, parts_ref.shape[0]):
        total = total + parts_ref[rep]
    rows = parts_ref.shape[2]
    per_half = rows // BLK
    start = rep_ref[0] * own
    for half in range(halves):
        block = lax.div(lax.broadcasted_iota(jnp.int32, (own, BLK), 0) + start, BLK)
        for across in range(rows // BLK):
            kept = jnp.zeros((own, BLK), jnp.float32)
            for down in range(per_half):
                keep = keep_ref[across, half * per_half + down].astype(jnp.float32)
                kept = jnp.where(block == down, keep, kept)
            at = slice(half * own, (half + 1) * own), slice(across * BLK, (across + 1) * BLK)
            square_ref[at] = total[at] * kept
    store_coded(low_ref, square_ref[...].astype(jnp.bfloat16).astype(jnp.float32))


def cube_part(own, halves, rep_ref, keep_ref, low_ref, right_ref, square_ref, out_ref, placed):
    rows = out_ref.shape[0]
    start = pl.multiple_of(rep_ref[0] * own, own)
    placed[...] = jnp.zeros_like(placed)
    for half in range(halves):
        placed[pl.ds(pl.multiple_of(half * rows + start, own), own), :] = (
            3.0 * square_ref[half * own : (half + 1) * own, :]
        )
    product = contract(low_ref[...], right_ref[...])
    for down in range(rows // BLK):
        for across in range(out_ref.shape[1] // BLK):
            at = slice(down * BLK, (down + 1) * BLK), slice(across * BLK, (across + 1) * BLK)
            factor = -2.0 * keep_ref[down, across].astype(jnp.float32)
            out_ref[at] = placed[at[1], at[0]].T + factor * product[at]


def local(density, keep_square, keep_cube):
    rows, cols = density.shape
    reps, col_count = lax.axis_size("rep"), lax.axis_size("col")
    own, halves = rows // reps, cols // rows
    rep = lax.axis_index("rep").astype(jnp.int32).reshape(1)
    shape = jax.ShapeDtypeStruct
    part = halves * own

    right_coded, left_copies = call(
        functools.partial(prepare, own, halves),
        (shape((own + HEAD, cols), jnp.bfloat16), shape((col_count, part, rows), jnp.bfloat16)),
        [SMEM, VMEM],
        [pltpu.VMEM((cols, rows), jnp.bfloat16)],
    )(rep, density)
    left = lax.all_to_all(left_copies, "col", 0, 0).reshape(col_count * part, rows)
    right = gather(right_coded, "row")
    parts = call(
        functools.partial(square_part, own, halves),
        shape((reps, part, rows), jnp.float32),
        [VMEM, VMEM],
    )(right, left)
    parts = lax.all_to_all(parts, "rep", 0, 0)
    square, low_coded = call(
        functools.partial(square_sum, own, halves),
        (shape((part, rows), jnp.float32), shape((part + HEAD, rows), jnp.bfloat16)),
        [SMEM, SMEM, VMEM],
    )(rep, keep_square, parts)
    low = gather(low_coded, "col")
    total = call(
        functools.partial(cube_part, own, halves),
        shape((rows, cols), jnp.float32),
        [SMEM, SMEM, VMEM, VMEM, VMEM],
        [pltpu.VMEM((cols, rows), jnp.float32)],
    )(rep, keep_cube, low, right, square)
    pieces = lax.all_to_all(total.reshape(reps, own, cols), "rep", 0, 0)
    return jnp.sum(pieces, axis=0)


def solution(mesh):
    return jax.shard_map(
        local,
        mesh=mesh,
        in_specs=(P("row", "col"), P("row", "col"), P("row", "col")),
        out_specs=P(("row", "rep"), "col"),
        check_vma=False,
    )
```

time: 415 us -> 118 us (0.28)
  waiting for transfers between devices: 368 us -> 0.01 us
  blocking collectives: 11 us -> 98.9 us
  between operations: 13.3 us -> 0.09 us
  starting transfers between devices: 0.17 us -> 10.3 us
  matrix products: 8.08 us -> 0 us
  other arithmetic: 7.85 us -> 1.66 us
  Pallas kernels: 0 us -> 5.29 us
  local copies, waits for them, and re-layouts: 5.4 us -> 1.13 us
    psum x3 -> x0, waiting for transfers between devices: 301 us -> none  [broadcast(): return lax.psum(jnp.where(mine, array, jnp.zeros_like(array)), axis)]
    reduce_scatter x2 -> x0, waiting for transfers between devices: 67.3 us -> none  [the longest x1 35.5 us: local(): lax.psum_scatter(square_total, 'rep', scatter_dimension=0, tiled=True)]
    all_gather x1 -> x2, blocking collectives: 11 us -> 65.8 us  [gather(): whole = lax.all_gather(coded.astype(jnp.float16), axis)]
    all_to_all x0 -> x2, blocking collectives: none -> 33.1 us  [the longest x1 18.7 us: local(): pieces = lax.all_to_all(total.reshape(reps, own, cols), 'rep', 0, 0)]
    all_to_all x0 -> x1, starting transfers between devices: none -> 10.3 us  [local(): lax.all_to_all(left_copies, 'col', 0, 0).reshape(col_count * part, rows)]
    dot_general x8 -> x0, matrix products: 8.08 us -> none  [the longest x4 4.15 us: local(): jnp.dot(left_piece(density, piece_index), right_panel, preferred_element_...]
    pallas_call x0 -> x4, Pallas kernels: none -> 5.29 us  [the longest x1 1.81 us: local(): call(functools.partial(cube_part, own, halves), shape((rows, cols), jnp.f...]
    select_n x3 -> x0, other arithmetic: 5.15 us -> none  [broadcast(): return lax.psum(jnp.where(mine, array, jnp.zeros_like(array)), axis)]
  transfers between devices with their start and end apart: 5 -> 1, of which waited for: 5 -> 0; matrix products, arithmetic and copies ran while one was open for 0% -> 1% of each run, Pallas kernels for 0% -> 0%
where the time goes in v2:
time: 118 us; the launch traced here: 117 us
  blocking collectives  98.9 us (84%)
  starting transfers between devices  10.3 us (9%)
  Pallas kernels  5.29 us (4%)
  other arithmetic  1.66 us (1%)
    all_gather x2, blocking collectives, gather(): whole = lax.all_gather(coded.astype(jnp.float16), axis)  65.8 us
    all_to_all x1, blocking collectives, local(): pieces = lax.all_to_all(total.reshape(reps, own, cols), 'rep', 0, 0)  18.7 us
    all_to_all x1, blocking collectives, local(): parts = lax.all_to_all(parts, 'rep', 0, 0)  14.4 us
    all_to_all x1, starting transfers between devices, local(): lax.all_to_all(left_copies, 'col', 0, 0).reshape(col_count * part, rows)  10.3 us
  transfers between devices with their start and end apart: 1, of which 0 were waited for; matrix products, arithmetic and copies ran while one was open for 1% of the time, Pallas kernels for 0%

profile of v2, /device:TPU:1, one launch (start us, length us, event | category | flops | bytes accessed | tf_op | source)
XLA Modules:
  0.0 117.4 jit_solution(2644476543964065880)
XLA Ops:
  0.0 0.0 copy-start
  0.0 1.1 copy-done
  1.1 1.3 %shard_map.37 = (bf16[104,768]{1,0:T(8,128)(2,1)S(1)}, bf16[8,192,384]{2,1,0:T(8,128)(2,1)}) custom-call(s32[1]{0:T(128)} %bitcast.rep_ref, bf16[384,768]{1,0:T(8,128)(2,1)S(1)} %copy-done), custom_call_target="tpu_custom_call" | custom-call | tf_op jit(solution)/shard_map/pallas_call | solution.py:121
  2.4 10.3 %all-to-all-start = ((bf16[8,192,384]{2,1,0:T(8,128)(2,1)}), bf16[8,192,384]{2,1,0:T(8,128)(2,1)S(1)}, u32[]{:S(2)}, u32[]{:S(2)}) async-start(bf16[8,192,384]{2,1,0:T(8,128)(2,1)} %get-tuple-element.10), calls=%async_computation | async-start | bytes 2359296 | tf_op jit(solution)/shard_map/all_to_all | solution.py:127
  12.8 43.3 %all-gather.4 = f16[1664,768]{1,0:T(8,128)(2,1)S(1)} all-gather(f16[104,768]{1,0:T(8,128)(2,1)S(1)} %convert_element_type.24), channel_id=2, replica_groups=mesh['row'=16,'col'=8,'rep'=4] {'row'}, dimensions={0}, use_global_device_ids=true | all-gather | bytes 2715648 | tf_op jit(solution)/shard_map/all_gather | solution.py:50
  56.2 0.5 multiply_convert_fusion
  56.7 0.0 all-to-all-done
  56.7 1.4 %shard_map.38 = f32[4,192,384]{2,1,0:T(8,128)S(1)} custom-call(bf16[1536,768]{1,0:T(8,128)(2,1)S(1)} %bitcast.11, bf16[1536,384]{1,0:T(8,128)(2,1)S(1)} %bitcast.13), custom_call_target="tpu_custom_call" | custom-call | tf_op jit(solution)/shard_map/pallas_call | solution.py:129
  58.1 0.0 copy-start.2
  58.1 14.4 %all_to_all.15.parts_ref = f32[4,192,384]{2,1,0:T(8,128)S(1)} all-to-all(f32[4,192,384]{2,1,0:T(8,128)S(1)} %shard_map.38), channel_id=1, replica_groups=mesh['row'=16,'col'=8,'rep'=4] {'rep'}, dimensions={0} | all-to-all | bytes 2359296 | tf_op jit(solution)/shard_map/all_to_all | solution.py:134
  72.6 0.0 copy-done.2
  72.6 0.0 copy-start.1
  72.6 0.7 shard_map.39
  73.4 22.5 %all-gather.5 = f16[1600,384]{1,0:T(8,128)(2,1)S(1)} all-gather(f16[200,384]{1,0:T(8,128)(2,1)S(1)} %convert_element_type.28), channel_id=3, replica_groups=mesh['row'=16,'col'=8,'rep'=4] {'col'}, dimensions={0}, use_global_device_ids=true | all-gather | bytes 1382400 | tf_op jit(solution)/shard_map/all_gather | solution.py:50
  95.9 0.2 multiply_convert_fusion.1
  96.1 0.0 copy-done.1
  96.1 1.8 %shard_map.40 = f32[384,768]{1,0:T(8,128)S(1)} custom-call(s32[1]{0:T(128)} %bitcast.rep_ref, s32[3,6]{1,0:T(4,128)S(1)} %copy-done.1, bf16[1536,384]{1,0:T(8,128)(2,1)S(1)} %bitcast.14, bf16[1536,768]{1,0:T(8,128)(2,1)S(1)} %bitcast.12, f32[192,384]{1,0:T(8,128)S(1)} %get-tuple-element.12.square_ref), custom_call_target="tpu_custom_call" | custom-call | tf_op jit(solution)/shard_map/pallas_call | solution.py:141
  98.0 18.7 %all_to_all.16 = f32[4,96,768]{2,1,0:T(8,128)S(1)} all-to-all(f32[4,96,768]{2,1,0:T(8,128)S(1)} %bitcast.15), channel_id=1, replica_groups=mesh['row'=16,'col'=8,'rep'=4] {'rep'}, dimensions={0} | all-to-all | bytes 2359296 | tf_op jit(solution)/shard_map/all_to_all | solution.py:147
  116.6 0.8 reduce_sum.9
  (6 shorter events, 0.1 us)
Async XLA Ops:
  0.0 1.1 copy-start
  2.4 54.3 %all-to-all-start = ((bf16[8,192,384]{2,1,0:T(8,128)(2,1)}), bf16[8,192,384]{2,1,0:T(8,128)(2,1)S(1)}, u32[]{:S(2)}, u32[]{:S(2)}) async-start(bf16[8,192,384]{2,1,0:T(8,128)(2,1)} %get-tuple-element.10), calls=%async_computation | async-start | bytes 2359296 | tf_op jit(solution)/shard_map/all_to_all | solution.py:127
  58.1 14.4 %copy-start.2 = (s32[3,6]{1,0:T(4,128)S(1)}, s32[3,6]{1,0:T(4,128)}, u32[]{:S(2)}) copy-start(s32[3,6]{1,0:T(4,128)} %keep_ref.2) | copy-start | bytes 220
  72.6 23.6 %copy-start.1 = (s32[3,6]{1,0:T(4,128)S(1)}, s32[3,6]{1,0:T(4,128)}, u32[]{:S(2)}) copy-start(s32[3,6]{1,0:T(4,128)} %keep_ref.3) | copy-start | bytes 220

commit v3 on v2

--- a/solution.py
+++ b/solution.py
@@ -40,19 +40,19 @@
 def store_coded(ref, values):
     coded, exponent = scaled(values)
     height = values.shape[0]
-    ref[:height, :] = coded.astype(jnp.bfloat16)
-    ref[height:, :] = jnp.broadcast_to(exponent, (ref.shape[0] - height, values.shape[1])).astype(
-        jnp.bfloat16
-    )
+    ref[:height, :] = coded.astype(ref.dtype)
+    ref[height:, :] = jnp.broadcast_to(exponent, (HEAD, values.shape[1])).astype(ref.dtype)
+
+
+def decode(pieces):
+    height = pieces.shape[1] - HEAD
+    scale = jnp.exp2(pieces[:, height : height + 1, :].astype(jnp.float32))
+    return pieces[:, :height, :].astype(jnp.float32) * (1.0 / TOP) * scale
 
 
 def gather(coded, axis):
-    whole = lax.all_gather(coded.astype(jnp.float16), axis)
-    count, height, width = whole.shape
-    height -= HEAD
-    scale = jnp.exp2(whole[:, height : height + 1, :].astype(jnp.float32))
-    values = whole[:, :height, :].astype(jnp.float32) * (1.0 / TOP) * scale
-    return values.astype(jnp.bfloat16).reshape(count * height, width)
+    values = decode(lax.all_gather(coded.astype(jnp.float16), axis)).astype(jnp.bfloat16)
+    return values.reshape(-1, values.shape[2])
 
 
 def prepare(own, halves, rep_ref, tile_ref, right_ref, left_ref, turned):
@@ -94,8 +94,8 @@
     store_coded(low_ref, square_ref[...].astype(jnp.bfloat16).astype(jnp.float32))
 
 
-def cube_part(own, halves, rep_ref, keep_ref, low_ref, right_ref, square_ref, out_ref, placed):
-    rows = out_ref.shape[0]
+def cube_part(own, halves, rep_ref, keep_ref, low_ref, right_ref, square_ref, out_ref, placed, total):
+    rows, cols = total.shape
     start = pl.multiple_of(rep_ref[0] * own, own)
     placed[...] = jnp.zeros_like(placed)
     for half in range(halves):
@@ -104,10 +104,12 @@
         )
     product = contract(low_ref[...], right_ref[...])
     for down in range(rows // BLK):
-        for across in range(out_ref.shape[1] // BLK):
+        for across in range(cols // BLK):
             at = slice(down * BLK, (down + 1) * BLK), slice(across * BLK, (across + 1) * BLK)
             factor = -2.0 * keep_ref[down, across].astype(jnp.float32)
-            out_ref[at] = placed[at[1], at[0]].T + factor * product[at]
+            total[at] = placed[at[1], at[0]].T + factor * product[at]
+    for rep in range(out_ref.shape[0]):
+        store_coded(out_ref.at[rep], total[rep * own : (rep + 1) * own, :])
 
 
 def local(density, keep_square, keep_cube):
@@ -140,12 +142,11 @@
     low = gather(low_coded, "col")
     total = call(
         functools.partial(cube_part, own, halves),
-        shape((rows, cols), jnp.float32),
+        shape((reps, own + HEAD, cols), jnp.float32),
         [SMEM, SMEM, VMEM, VMEM, VMEM],
-        [pltpu.VMEM((cols, rows), jnp.float32)],
+        [pltpu.VMEM((cols, rows), jnp.float32), pltpu.VMEM((rows, cols), jnp.float32)],
     )(rep, keep_cube, low, right, square)
-    pieces = lax.all_to_all(total.reshape(reps, own, cols), "rep", 0, 0)
-    return jnp.sum(pieces, axis=0)
+    return jnp.sum(decode(lax.all_to_all(total.astype(jnp.float16), "rep", 0, 0)), axis=0)
 
 
 def solution(mesh):

time: 118 us -> 113 us (0.958)
  blocking collectives: 98.9 us -> 93.3 us
    all_to_all x1, blocking collectives: 18.7 us -> 13 us  [local(): lax.all_to_all(total.astype(jnp.float16), 'rep', 0, 0)]
where the time goes in v3:
time: 113 us; the launch traced here: 112 us
  blocking collectives  93.3 us (83%)
  starting transfers between devices  10.3 us (9%)
  Pallas kernels  5.4 us (5%)
  other arithmetic  1.8 us (2%)
  local copies, waits for them, and re-layouts  1.53 us (1%)
    all_gather x2, blocking collectives, gather(): lax.all_gather(coded.astype(jnp.float16), axis)  65.8 us
    all_to_all x1, blocking collectives, local(): parts = lax.all_to_all(parts, 'rep', 0, 0)  14.4 us
    all_to_all x1, blocking collectives, local(): lax.all_to_all(total.astype(jnp.float16), 'rep', 0, 0)  13 us
    all_to_all x1, starting transfers between devices, local(): lax.all_to_all(left_copies, 'col', 0, 0).reshape(col_count * part, rows)  10.3 us
  transfers between devices with their start and end apart: 1, of which 0 were waited for; matrix products, arithmetic and copies ran while one was open for 1% of the time, Pallas kernels for 0%

profile of v3, /device:TPU:1, one launch (start us, length us, event | category | flops | bytes accessed | tf_op | source)
XLA Modules:
  0.0 112.4 jit_solution(8579555628653604314)
XLA Ops:
  0.0 0.0 copy-start
  0.0 1.1 copy-done
  1.1 1.3 %shard_map.37 = (bf16[104,768]{1,0:T(8,128)(2,1)S(1)}, bf16[8,192,384]{2,1,0:T(8,128)(2,1)}) custom-call(s32[1]{0:T(128)} %bitcast.rep_ref, bf16[384,768]{1,0:T(8,128)(2,1)S(1)} %copy-done), custom_call_target="tpu_custom_call" | custom-call | tf_op jit(solution)/shard_map/pallas_call | solution.py:123
  2.4 10.3 %all-to-all-start = ((bf16[8,192,384]{2,1,0:T(8,128)(2,1)}), bf16[8,192,384]{2,1,0:T(8,128)(2,1)S(1)}, u32[]{:S(2)}, u32[]{:S(2)}) async-start(bf16[8,192,384]{2,1,0:T(8,128)(2,1)} %get-tuple-element.10), calls=%async_computation | async-start | bytes 2359296 | tf_op jit(solution)/shard_map/all_to_all | solution.py:129
  12.8 43.3 %all-gather.4 = f16[1664,768]{1,0:T(8,128)(2,1)S(1)} all-gather(f16[104,768]{1,0:T(8,128)(2,1)S(1)} %convert_element_type.33), channel_id=2, replica_groups=mesh['row'=16,'col'=8,'rep'=4] {'row'}, dimensions={0}, use_global_device_ids=true | all-gather | bytes 2715648 | tf_op jit(solution)/shard_map/all_gather | solution.py:54
  56.2 0.5 multiply_convert_fusion
  56.7 0.0 all-to-all-done
  56.7 1.4 %shard_map.38 = f32[4,192,384]{2,1,0:T(8,128)S(1)} custom-call(bf16[1536,768]{1,0:T(8,128)(2,1)S(1)} %bitcast.13, bf16[1536,384]{1,0:T(8,128)(2,1)S(1)} %bitcast.16), custom_call_target="tpu_custom_call" | custom-call | tf_op jit(solution)/shard_map/pallas_call | solution.py:131
  58.1 0.0 copy-start.2
  58.1 14.4 %all_to_all.15.parts_ref = f32[4,192,384]{2,1,0:T(8,128)S(1)} all-to-all(f32[4,192,384]{2,1,0:T(8,128)S(1)} %shard_map.38), channel_id=1, replica_groups=mesh['row'=16,'col'=8,'rep'=4] {'rep'}, dimensions={0} | all-to-all | bytes 2359296 | tf_op jit(solution)/shard_map/all_to_all | solution.py:136
  72.6 0.0 copy-done.2
  72.6 0.7 shard_map.39
  73.4 22.5 %all-gather.5 = f16[1600,384]{1,0:T(8,128)(2,1)S(1)} all-gather(f16[200,384]{1,0:T(8,128)(2,1)S(1)} %convert_element_type.37), channel_id=3, replica_groups=mesh['row'=16,'col'=8,'rep'=4] {'col'}, dimensions={0}, use_global_device_ids=true | all-gather | bytes 1382400 | tf_op jit(solution)/shard_map/all_gather | solution.py:54
  95.8 0.0 copy-start.1
  95.9 0.2 multiply_convert_fusion.1
  96.1 0.4 copy-done.1
  96.5 1.9 %shard_map.40 = f32[4,104,768]{2,1,0:T(8,128)S(1)} custom-call(s32[1]{0:T(128)} %bitcast.rep_ref, s32[3,6]{1,0:T(4,128)S(1)} %copy-done.1, bf16[1536,384]{1,0:T(8,128)(2,1)S(1)} %bitcast.15, bf16[1536,768]{1,0:T(8,128)(2,1)S(1)} %bitcast.14, f32[192,384]{1,0:T(8,128)S(1)} %get-tuple-element.12.square_ref), custom_call_target="tpu_custom_call" | custom-call | tf_op jit(solution)/shard_map/pallas_call | solution.py:143
  98.5 0.1 convert_element_type.41
  98.5 13.0 %all_to_all.16 = f16[4,104,768]{2,1,0:T(8,128)(2,1)S(1)} all-to-all(f16[4,104,768]{2,1,0:T(8,128)(2,1)S(1)} %convert_element_type.41), channel_id=1, replica_groups=mesh['row'=16,'col'=8,'rep'=4] {'rep'}, dimensions={0} | all-to-all | bytes 1277952 | tf_op jit(solution)/shard_map/all_to_all | solution.py:149
  111.6 0.8 multiply_reduce_fusion
  (8 shorter events, 0.2 us)
Async XLA Ops:
  0.0 1.1 copy-start
  2.4 54.3 %all-to-all-start = ((bf16[8,192,384]{2,1,0:T(8,128)(2,1)}), bf16[8,192,384]{2,1,0:T(8,128)(2,1)S(1)}, u32[]{:S(2)}, u32[]{:S(2)}) async-start(bf16[8,192,384]{2,1,0:T(8,128)(2,1)} %get-tuple-element.10), calls=%async_computation | async-start | bytes 2359296 | tf_op jit(solution)/shard_map/all_to_all | solution.py:129
  58.1 14.4 %copy-start.2 = (s32[3,6]{1,0:T(4,128)S(1)}, s32[3,6]{1,0:T(4,128)}, u32[]{:S(2)}) copy-start(s32[3,6]{1,0:T(4,128)} %keep_ref.2) | copy-start | bytes 220
  95.8 0.7 copy-start.1

commit v4 on v3

--- a/solution.py
+++ b/solution.py
@@ -22,7 +22,7 @@
         out_shape=out_shape,
         in_specs=in_specs,
         scratch_shapes=list(scratch),
-        compiler_params=pltpu.CompilerParams(vmem_limit_bytes=48 << 20),
+        compiler_params=pltpu.CompilerParams(vmem_limit_bytes=32 << 20),
     )
 
 
@@ -44,29 +44,63 @@
     ref[height:, :] = jnp.broadcast_to(exponent, (HEAD, values.shape[1])).astype(ref.dtype)
 
 
+def store_packed(ref, values):
+    coded, exponent = scaled(values)
+    height, width = values.shape
+    groups = width // BLK
+    for group in range(groups):
+        columns = slice(group * BLK, (group + 1) * BLK)
+        ref[group * height : (group + 1) * height, :] = coded[:, columns].astype(ref.dtype)
+    rows = [exponent[:, group * BLK : (group + 1) * BLK] for group in range(groups)]
+    rows.append(jnp.zeros((HEAD - groups, BLK), jnp.float32))
+    ref[groups * height :, :] = jnp.concatenate(rows, axis=0).astype(ref.dtype)
+
+
 def decode(pieces):
     height = pieces.shape[1] - HEAD
     scale = jnp.exp2(pieces[:, height : height + 1, :].astype(jnp.float32))
     return pieces[:, :height, :].astype(jnp.float32) * (1.0 / TOP) * scale
 
 
-def gather(coded, axis):
-    values = decode(lax.all_gather(coded.astype(jnp.float16), axis)).astype(jnp.bfloat16)
-    return values.reshape(-1, values.shape[2])
-
-
-def prepare(own, halves, rep_ref, tile_ref, right_ref, left_ref, turned):
+def gather(packed, axis):
+    return lax.all_gather(packed.astype(jnp.float16), axis).astype(jnp.bfloat16)
+
+
+def panel(ref, groups):
+    count, height, _ = ref.shape
+    height = (height - HEAD) // groups
+    scale = jnp.exp2(ref[:, groups * height :, :].astype(jnp.float32)) * (1.0 / TOP)
+    columns = []
+    for group in range(groups):
+        values = ref[:, group * height : (group + 1) * height, :].astype(jnp.float32)
+        values = values * scale[:, group : group + 1, :]
+        columns.append(values.astype(jnp.bfloat16).reshape(count * height, BLK))
+    return jnp.concatenate(columns, axis=1)
+
+
+def prepare(own, halves, rep_ref, tile_ref, right_ref, left_ref, tile, turned, arrived):
     rows = tile_ref.shape[0]
+    copies = [
+        pltpu.make_async_copy(
+            tile_ref.at[pl.ds(part * own, own), :], tile.at[pl.ds(part * own, own), :], arrived.at[part]
+        )
+        for part in range(rows // own)
+    ]
+    for copy in copies:
+        copy.start()
+    for copy in copies:
+        copy.wait()
     start = pl.multiple_of(rep_ref[0] * own, own)
-    store_coded(right_ref, tile_ref[pl.ds(start, own), :].astype(jnp.float32))
-    turned[...] = tile_ref[...].T
+    store_packed(right_ref, tile[pl.ds(start, own), :].astype(jnp.float32))
+    turned[...] = tile[...].T
     for half in range(halves):
         piece = turned[pl.ds(pl.multiple_of(half * rows + start, own), own), :]
         for to in range(left_ref.shape[0]):
             left_ref[to, half * own : (half + 1) * own, :] = piece
 
 
-def square_part(own, halves, right_ref, left_ref, out_ref):
+def square_part(own, halves, packed_ref, left_ref, out_ref, right_ref):
+    right_ref[...] = panel(packed_ref, right_ref.shape[1] // BLK)
     product = contract(right_ref[...], left_ref[...])
     rows = product.shape[0] // halves
     for rep in range(out_ref.shape[0]):
@@ -91,7 +125,7 @@
                 kept = jnp.where(block == down, keep, kept)
             at = slice(half * own, (half + 1) * own), slice(across * BLK, (across + 1) * BLK)
             square_ref[at] = total[at] * kept
-    store_coded(low_ref, square_ref[...].astype(jnp.bfloat16).astype(jnp.float32))
+    store_packed(low_ref, square_ref[...].astype(jnp.bfloat16).astype(jnp.float32))
 
 
 def cube_part(own, halves, rep_ref, keep_ref, low_ref, right_ref, square_ref, out_ref, placed, total):
@@ -102,7 +136,7 @@
         placed[pl.ds(pl.multiple_of(half * rows + start, own), own), :] = (
             3.0 * square_ref[half * own : (half + 1) * own, :]
         )
-    product = contract(low_ref[...], right_ref[...])
+    product = contract(panel(low_ref, rows // BLK), right_ref[...])
     for down in range(rows // BLK):
         for across in range(cols // BLK):
             at = slice(down * BLK, (down + 1) * BLK), slice(across * BLK, (across + 1) * BLK)
@@ -122,21 +156,34 @@
 
     right_coded, left_copies = call(
         functools.partial(prepare, own, halves),
-        (shape((own + HEAD, cols), jnp.bfloat16), shape((col_count, part, rows), jnp.bfloat16)),
-        [SMEM, VMEM],
-        [pltpu.VMEM((cols, rows), jnp.bfloat16)],
-    )(rep, density)
+        (
+            shape((own * (cols // BLK) + HEAD, BLK), jnp.bfloat16),
+            shape((col_count, part, rows), jnp.bfloat16),
+        ),
+        [SMEM, pl.BlockSpec(memory_space=pltpu.HBM)],
+        [
+            pltpu.VMEM((rows, cols), jnp.bfloat16),
+            pltpu.VMEM((cols, rows), jnp.bfloat16),
+            pltpu.SemaphoreType.DMA((reps,)),
+        ],
+    )(rep, pltpu.with_memory_space_constraint(density, pltpu.HBM))
     left = lax.all_to_all(left_copies, "col", 0, 0).reshape(col_count * part, rows)
     right = gather(right_coded, "row")
-    parts = call(
+    parts, right = call(
         functools.partial(square_part, own, halves),
-        shape((reps, part, rows), jnp.float32),
+        (
+            shape((reps, part, rows), jnp.float32),
+            shape((right.shape[0] * own, cols), jnp.bfloat16),
+        ),
         [VMEM, VMEM],
     )(right, left)
     parts = lax.all_to_all(parts, "rep", 0, 0)
     square, low_coded = call(
         functools.partial(square_sum, own, halves),
-        (shape((part, rows), jnp.float32), shape((part + HEAD, rows), jnp.bfloat16)),
+        (
+            shape((part, rows), jnp.float32),
+            shape((part * (rows // BLK) + HEAD, BLK), jnp.bfloat16),
+        ),
         [SMEM, SMEM, VMEM],
     )(rep, keep_square, parts)
     low = gather(low_coded, "col")

time: 113 us -> 112 us (level)
  Pallas kernels: 5.4 us -> 7.91 us
  blocking collectives: 93.3 us -> 91 us
    pallas_call x2, Pallas kernels: 2.74 us -> 5.2 us  [the longest x1 2.7 us: local(): call(functools.partial(square_part, own, halves), (shape((reps, part, row...]
    all_gather x2, blocking collectives: 65.8 us -> 63.5 us  [gather(): return lax.all_gather(packed.astype(jnp.float16), axis).astype(jnp.bfloat16)]
  transfers between devices with their start and end apart: 1 -> 1, of which waited for: 0 -> 0; matrix products, arithmetic and copies ran while one was open for 1% -> 0% of each run, Pallas kernels for 0% -> 0%
where the time goes in v4:
time: 112 us
  blocking collectives  91 us (81%)
  starting transfers between devices  11 us (10%)
  Pallas kernels  7.91 us (7%)
  other arithmetic  1.42 us (1%)
    all_gather x2, blocking collectives, gather(): return lax.all_gather(packed.astype(jnp.float16), axis).astype(jnp.bfloat16)  63.5 us
    all_to_all x1, blocking collectives, local(): parts = lax.all_to_all(parts, 'rep', 0, 0)  14.5 us
    all_to_all x1, blocking collectives, local(): lax.all_to_all(total.astype(jnp.float16), 'rep', 0, 0)  13 us
    all_to_all x1, starting transfers between devices, local(): lax.all_to_all(left_copies, 'col', 0, 0).reshape(col_count * part, rows)  11 us
    pallas_call x1, Pallas kernels, local(): call(functools.partial(square_part, own, halves), (shape((reps, part, row...  2.7 us
    pallas_call x1, Pallas kernels, local(): call(functools.partial(prepare, own, halves), (shape((own * (cols // BLK)...  2.49 us
  transfers between devices with their start and end apart: 1, of which 0 were waited for; matrix products, arithmetic and copies ran while one was open for 0% of the time, Pallas kernels for 0%

profile of v4, /device:TPU:1, one launch (start us, length us, event | category | flops | bytes accessed | tf_op | source)
XLA Modules:
  0.0 111.9 jit_solution(4889958608884270760)
XLA Ops:
  0.0 2.5 %shard_map.37 = (bf16[584,128]{1,0:T(8,128)(2,1)S(1)}, bf16[8,192,384]{2,1,0:T(8,128)(2,1)}) custom-call(s32[1]{0:T(128)} %bitcast.rep_ref, bf16[384,768]{1,0:T(8,128)(2,1)} %tile_ref.1), custom_call_target="tpu_custom_call" | custom-call | tf_op jit(solution)/shard_map/pallas_call | solution.py:157
  2.5 11.0 %all-to-all-start = ((bf16[8,192,384]{2,1,0:T(8,128)(2,1)}), bf16[8,192,384]{2,1,0:T(8,128)(2,1)}, u32[]{:S(2)}, u32[]{:S(2)}) async-start(bf16[8,192,384]{2,1,0:T(8,128)(2,1)} %get-tuple-element.12), calls=%async_computation | async-start | bytes 2359296 | tf_op jit(solution)/shard_map/all_to_all | solution.py:170
  13.6 41.6 %all-gather.4 = f16[9344,128]{1,0:T(8,128)(2,1)S(1)} all-gather(f16[584,128]{1,0:T(8,128)(2,1)S(1)} %convert_element_type.21), channel_id=2, replica_groups=mesh['row'=16,'col'=8,'rep'=4] {'row'}, dimensions={0}, use_global_device_ids=true | all-gather | bytes 2541568 | tf_op jit(solution)/shard_map/all_gather | solution.py:66
  55.1 0.3 convert_element_type.28
  55.4 0.0 all-to-all-done
  55.4 2.7 %shard_map.38 = (f32[4,192,384]{2,1,0:T(8,128)S(1)}, bf16[1536,768]{1,0:T(8,128)(2,1)S(1)}) custom-call(bf16[16,584,128]{2,1,0:T(8,128)(2,1)S(1)} %bitcast.7, bf16[1536,384]{1,0:T(8,128)(2,1)} %bitcast.2.left_ref), custom_call_target="tpu_custom_call" | custom-call | tf_op jit(solution)/shard_map/pallas_call | solution.py:172
  58.1 0.0 copy-start.1
  58.1 14.5 %all_to_all.15.parts_ref = f32[4,192,384]{2,1,0:T(8,128)S(1)} all-to-all(f32[4,192,384]{2,1,0:T(8,128)S(1)} %get-tuple-element.13), channel_id=1, replica_groups=mesh['row'=16,'col'=8,'rep'=4] {'rep'}, dimensions={0} | all-to-all | bytes 2359296 | tf_op jit(solution)/shard_map/all_to_all | solution.py:180
  72.6 0.0 copy-done.1
  72.6 0.7 shard_map.39
  73.4 21.9 %all-gather.5 = f16[4672,128]{1,0:T(8,128)(2,1)S(1)} all-gather(f16[584,128]{1,0:T(8,128)(2,1)S(1)} %convert_element_type.23), channel_id=3, replica_groups=mesh['row'=16,'col'=8,'rep'=4] {'col'}, dimensions={0}, use_global_device_ids=true | all-gather | bytes 1345536 | tf_op jit(solution)/shard_map/all_gather | solution.py:66
  95.3 0.0 copy-start
  95.3 0.1 convert_element_type.29
  95.4 0.5 copy-done
  96.0 2.0 %shard_map.40 = f32[4,104,768]{2,1,0:T(8,128)S(1)} custom-call(s32[1]{0:T(128)} %bitcast.rep_ref, s32[3,6]{1,0:T(4,128)S(1)} %copy-done, bf16[8,584,128]{2,1,0:T(8,128)(2,1)S(1)} %bitcast.8, bf16[1536,768]{1,0:T(8,128)(2,1)S(1)} %get-tuple-element.15.right_ref, f32[192,384]{1,0:T(8,128)S(1)} %get-tuple-element.16.square_ref), custom_call_target="tpu_custom_call" | custom-call | tf_op jit(solution)/shard_map/pallas_call | solution.py:190
  98.0 0.1 convert_element_type.25
  98.1 13.0 %all_to_all.16 = f16[4,104,768]{2,1,0:T(8,128)(2,1)S(1)} all-to-all(f16[4,104,768]{2,1,0:T(8,128)(2,1)S(1)} %convert_element_type.25), channel_id=1, replica_groups=mesh['row'=16,'col'=8,'rep'=4] {'rep'}, dimensions={0} | all-to-all | bytes 1277952 | tf_op jit(solution)/shard_map/all_to_all | solution.py:196
  111.1 0.8 multiply_reduce_fusion
  (4 shorter events, 0.1 us)
Async XLA Ops:
  2.5 52.9 %all-to-all-start = ((bf16[8,192,384]{2,1,0:T(8,128)(2,1)}), bf16[8,192,384]{2,1,0:T(8,128)(2,1)}, u32[]{:S(2)}, u32[]{:S(2)}) async-start(bf16[8,192,384]{2,1,0:T(8,128)(2,1)} %get-tuple-element.12), calls=%async_computation | async-start | bytes 2359296 | tf_op jit(solution)/shard_map/all_to_all | solution.py:170
  58.1 14.5 %copy-start.1 = (s32[3,6]{1,0:T(4,128)S(1)}, s32[3,6]{1,0:T(4,128)}, u32[]{:S(2)}) copy-start(s32[3,6]{1,0:T(4,128)} %keep_ref.2) | copy-start | bytes 220
  95.3 0.7 copy-start

commit v5 on v4

--- a/solution.py
+++ b/solution.py
@@ -14,6 +14,7 @@
 
 SMEM = pl.BlockSpec(memory_space=pltpu.SMEM)
 VMEM = pl.BlockSpec(memory_space=pltpu.VMEM)
+HBM = pl.BlockSpec(memory_space=pltpu.HBM)
 
 
 def call(kernel, out_shape, in_specs, scratch=()):
@@ -99,9 +100,12 @@
             left_ref[to, half * own : (half + 1) * own, :] = piece
 
 
-def square_part(own, halves, packed_ref, left_ref, out_ref, right_ref):
+def square_part(own, halves, packed_ref, left_ref, out_ref, right_ref, left, arrived):
+    load = pltpu.make_async_copy(left_ref, left, arrived)
+    load.start()
     right_ref[...] = panel(packed_ref, right_ref.shape[1] // BLK)
-    product = contract(right_ref[...], left_ref[...])
+    load.wait()
+    product = contract(right_ref[...], left[...])
     rows = product.shape[0] // halves
     for rep in range(out_ref.shape[0]):
         for half in range(halves):
@@ -109,7 +113,7 @@
             out_ref[rep, half * own : (half + 1) * own, :] = product[first : first + own, :]
 
 
-def square_sum(own, halves, rep_ref, keep_ref, parts_ref, square_ref, low_ref):
+def square_sum(own, halves, rep_ref, keep_ref, later_ref, parts_ref, square_ref, low_ref, factor_ref):
     total = parts_ref[0]
     for rep in range(1, parts_ref.shape[0]):
         total = total + parts_ref[rep]
@@ -125,10 +129,14 @@
                 kept = jnp.where(block == down, keep, kept)
             at = slice(half * own, (half + 1) * own), slice(across * BLK, (across + 1) * BLK)
             square_ref[at] = total[at] * kept
+    for down in range(later_ref.shape[0]):
+        for across in range(later_ref.shape[1]):
+            factor = -2.0 * later_ref[down, across].astype(jnp.float32)
+            factor_ref[down, :, across * BLK : (across + 1) * BLK] = jnp.full((8, BLK), factor)
     store_packed(low_ref, square_ref[...].astype(jnp.bfloat16).astype(jnp.float32))
 
 
-def cube_part(own, halves, rep_ref, keep_ref, low_ref, right_ref, square_ref, out_ref, placed, total):
+def cube_part(own, halves, rep_ref, factor_ref, low_ref, right_ref, square_ref, out_ref, placed, total):
     rows, cols = total.shape
     start = pl.multiple_of(rep_ref[0] * own, own)
     placed[...] = jnp.zeros_like(placed)
@@ -140,8 +148,7 @@
     for down in range(rows // BLK):
         for across in range(cols // BLK):
             at = slice(down * BLK, (down + 1) * BLK), slice(across * BLK, (across + 1) * BLK)
-            factor = -2.0 * keep_ref[down, across].astype(jnp.float32)
-            total[at] = placed[at[1], at[0]].T + factor * product[at]
+            total[at] = placed[at[1], at[0]].T + factor_ref[down, :1, at[1]] * product[at]
     for rep in range(out_ref.shape[0]):
         store_coded(out_ref.at[rep], total[rep * own : (rep + 1) * own, :])
 
@@ -160,7 +167,7 @@
             shape((own * (cols // BLK) + HEAD, BLK), jnp.bfloat16),
             shape((col_count, part, rows), jnp.bfloat16),
         ),
-        [SMEM, pl.BlockSpec(memory_space=pltpu.HBM)],
+        [SMEM, HBM],
         [
             pltpu.VMEM((rows, cols), jnp.bfloat16),
             pltpu.VMEM((cols, rows), jnp.bfloat16),
@@ -168,6 +175,7 @@
         ],
     )(rep, pltpu.with_memory_space_constraint(density, pltpu.HBM))
     left = lax.all_to_all(left_copies, "col", 0, 0).reshape(col_count * part, rows)
+    left = pltpu.with_memory_space_constraint(left, pltpu.HBM)
     right = gather(right_coded, "row")
     parts, right = call(
         functools.partial(square_part, own, halves),
@@ -175,24 +183,26 @@
             shape((reps, part, rows), jnp.float32),
             shape((right.shape[0] * own, cols), jnp.bfloat16),
         ),
-        [VMEM, VMEM],
+        [VMEM, HBM],
+        [pltpu.VMEM(left.shape, left.dtype), pltpu.SemaphoreType.DMA],
     )(right, left)
     parts = lax.all_to_all(parts, "rep", 0, 0)
-    square, low_coded = call(
+    square, low_coded, factor = call(
         functools.partial(square_sum, own, halves),
         (
             shape((part, rows), jnp.float32),
             shape((part * (rows // BLK) + HEAD, BLK), jnp.bfloat16),
+            shape((rows // BLK, 8, cols), jnp.float32),
         ),
-        [SMEM, SMEM, VMEM],
-    )(rep, keep_square, parts)
+        [SMEM, SMEM, SMEM, VMEM],
+    )(rep, keep_square, keep_cube, parts)
     low = gather(low_coded, "col")
     total = call(
         functools.partial(cube_part, own, halves),
         shape((reps, own + HEAD, cols), jnp.float32),
-        [SMEM, SMEM, VMEM, VMEM, VMEM],
+        [SMEM, VMEM, VMEM, VMEM, VMEM],
         [pltpu.VMEM((cols, rows), jnp.float32), pltpu.VMEM((rows, cols), jnp.float32)],
-    )(rep, keep_cube, low, right, square)
+    )(rep, factor, low, right, square)
     return jnp.sum(decode(lax.all_to_all(total.astype(jnp.float16), "rep", 0, 0)), axis=0)
 
 

time: 112 us -> 111 us (level)
  no operation moved by 1% of the time
where the time goes in v5:
time: 111 us
  blocking collectives  91 us (82%)
  starting transfers between devices  11 us (10%)
  Pallas kernels  7.36 us (7%)
  other arithmetic  1.42 us (1%)
    all_gather x2, blocking collectives, gather(): return lax.all_gather(packed.astype(jnp.float16), axis).astype(jnp.bfloat16)  63.5 us
    all_to_all x1, blocking collectives, local(): parts = lax.all_to_all(parts, 'rep', 0, 0)  14.5 us
    all_to_all x1, blocking collectives, local(): lax.all_to_all(total.astype(jnp.float16), 'rep', 0, 0)  13 us
    all_to_all x1, starting transfers between devices, local(): lax.all_to_all(left_copies, 'col', 0, 0).reshape(col_count * part, rows)  11 us
    pallas_call x1, Pallas kernels, local(): call(functools.partial(square_part, own, halves), (shape((reps, part, row...  2.7 us
    pallas_call x1, Pallas kernels, local(): call(functools.partial(prepare, own, halves), (shape((own * (cols // BLK)...  2.49 us
  transfers between devices with their start and end apart: 1, of which 0 were waited for; matrix products, arithmetic and copies ran while one was open for 0% of the time, Pallas kernels for 0%

profile of v5, /device:TPU:1, one launch (start us, length us, event | category | flops | bytes accessed | tf_op | source)
XLA Modules:
  0.0 110.9 jit_solution(10601404567441667537)
XLA Ops:
  0.0 2.5 %shard_map.37 = (bf16[584,128]{1,0:T(8,128)(2,1)S(1)}, bf16[8,192,384]{2,1,0:T(8,128)(2,1)}) custom-call(s32[1]{0:T(128)} %bitcast.rep_ref, bf16[384,768]{1,0:T(8,128)(2,1)} %tile_ref.1), custom_call_target="tpu_custom_call" | custom-call | tf_op jit(solution)/shard_map/pallas_call | solution.py:164
  2.5 11.0 %all-to-all-start = ((bf16[8,192,384]{2,1,0:T(8,128)(2,1)}), bf16[8,192,384]{2,1,0:T(8,128)(2,1)}, u32[]{:S(2)}, u32[]{:S(2)}) async-start(bf16[8,192,384]{2,1,0:T(8,128)(2,1)} %get-tuple-element.13), calls=%async_computation | async-start | bytes 2359296 | tf_op jit(solution)/shard_map/all_to_all | solution.py:177
  13.6 41.6 %all-gather.4 = f16[9344,128]{1,0:T(8,128)(2,1)S(1)} all-gather(f16[584,128]{1,0:T(8,128)(2,1)S(1)} %convert_element_type.21), channel_id=2, replica_groups=mesh['row'=16,'col'=8,'rep'=4] {'row'}, dimensions={0}, use_global_device_ids=true | all-gather | bytes 2541568 | tf_op jit(solution)/shard_map/all_gather | solution.py:67
  55.1 0.3 convert_element_type.28
  55.4 0.0 all-to-all-done
  55.4 2.7 %shard_map.38 = (f32[4,192,384]{2,1,0:T(8,128)S(1)}, bf16[1536,768]{1,0:T(8,128)(2,1)S(1)}) custom-call(bf16[16,584,128]{2,1,0:T(8,128)(2,1)S(1)} %bitcast.7, bf16[1536,384]{1,0:T(8,128)(2,1)} %bitcast.2.left_ref), custom_call_target="tpu_custom_call" | custom-call | tf_op jit(solution)/shard_map/pallas_call | solution.py:180
  58.1 0.0 copy-start
  58.1 0.0 copy-start.1
  58.2 14.5 %all_to_all.15.parts_ref = f32[4,192,384]{2,1,0:T(8,128)S(1)} all-to-all(f32[4,192,384]{2,1,0:T(8,128)S(1)} %get-tuple-element.14), channel_id=1, replica_groups=mesh['row'=16,'col'=8,'rep'=4] {'rep'}, dimensions={0} | all-to-all | bytes 2359296 | tf_op jit(solution)/shard_map/all_to_all | solution.py:189
  72.6 0.0 copy-done
  72.6 0.0 copy-done.1
  72.6 0.8 shard_map.39
  73.4 21.9 %all-gather.5 = f16[4672,128]{1,0:T(8,128)(2,1)S(1)} all-gather(f16[584,128]{1,0:T(8,128)(2,1)S(1)} %convert_element_type.23), channel_id=3, replica_groups=mesh['row'=16,'col'=8,'rep'=4] {'col'}, dimensions={0}, use_global_device_ids=true | all-gather | bytes 1345536 | tf_op jit(solution)/shard_map/all_gather | solution.py:67
  95.4 0.1 convert_element_type.29
  95.5 1.4 %shard_map.40 = f32[4,104,768]{2,1,0:T(8,128)S(1)} custom-call(s32[1]{0:T(128)} %bitcast.rep_ref, f32[3,8,768]{2,1,0:T(8,128)S(1)} %get-tuple-element.15.factor_ref, bf16[8,584,128]{2,1,0:T(8,128)(2,1)S(1)} %bitcast.8, bf16[1536,768]{1,0:T(8,128)(2,1)S(1)} %get-tuple-element.17.right_ref, f32[192,384]{1,0:T(8,128)S(1)} %get-tuple-element.18.square_ref), custom_call_target="tpu_custom_call" | custom-call | tf_op jit(solution)/shard_map/pallas_call | solution.py:200
  96.9 0.1 convert_element_type.25
  97.0 13.0 %all_to_all.16 = f16[4,104,768]{2,1,0:T(8,128)(2,1)S(1)} all-to-all(f16[4,104,768]{2,1,0:T(8,128)(2,1)S(1)} %convert_element_type.25), channel_id=1, replica_groups=mesh['row'=16,'col'=8,'rep'=4] {'rep'}, dimensions={0} | all-to-all | bytes 1277952 | tf_op jit(solution)/shard_map/all_to_all | solution.py:206
  110.0 0.8 multiply_reduce_fusion
  (4 shorter events, 0.1 us)
Async XLA Ops:
  2.5 52.9 %all-to-all-start = ((bf16[8,192,384]{2,1,0:T(8,128)(2,1)}), bf16[8,192,384]{2,1,0:T(8,128)(2,1)}, u32[]{:S(2)}, u32[]{:S(2)}) async-start(bf16[8,192,384]{2,1,0:T(8,128)(2,1)} %get-tuple-element.13), calls=%async_computation | async-start | bytes 2359296 | tf_op jit(solution)/shard_map/all_to_all | solution.py:177
  58.1 14.5 %copy-start = (s32[3,6]{1,0:T(4,128)S(1)}, s32[3,6]{1,0:T(4,128)}, u32[]{:S(2)}) copy-start(s32[3,6]{1,0:T(4,128)} %keep_ref.1) | copy-start | bytes 220
  58.1 14.5 %copy-start.1 = (s32[3,6]{1,0:T(4,128)S(1)}, s32[3,6]{1,0:T(4,128)}, u32[]{:S(2)}) copy-start(s32[3,6]{1,0:T(4,128)} %later_ref.1) | copy-start | bytes 220

commit v6 on v5

--- a/solution.py
+++ b/solution.py
@@ -63,19 +63,22 @@
     return pieces[:, :height, :].astype(jnp.float32) * (1.0 / TOP) * scale
 
 
-def gather(packed, axis):
-    return lax.all_gather(packed.astype(jnp.float16), axis).astype(jnp.bfloat16)
+def gather(packed, axis, groups):
+    whole = lax.all_gather(packed.astype(jnp.float16), axis)
+    count, height = whole.shape[0], whole.shape[1] - HEAD
+    scale = jnp.exp2(whole[:, height : height + groups, :].astype(jnp.float32)) * (1.0 / TOP)
+    scale = jnp.broadcast_to(scale[:, :, None, :], (count, groups, height // groups, BLK))
+    values = whole[:, :height, :].astype(jnp.float32) * scale.reshape(count, height, BLK)
+    return values.astype(jnp.bfloat16)
 
 
 def panel(ref, groups):
     count, height, _ = ref.shape
-    height = (height - HEAD) // groups
-    scale = jnp.exp2(ref[:, groups * height :, :].astype(jnp.float32)) * (1.0 / TOP)
-    columns = []
-    for group in range(groups):
-        values = ref[:, group * height : (group + 1) * height, :].astype(jnp.float32)
-        values = values * scale[:, group : group + 1, :]
-        columns.append(values.astype(jnp.bfloat16).reshape(count * height, BLK))
+    height //= groups
+    columns = [
+        ref[:, group * height : (group + 1) * height, :].reshape(count * height, BLK)
+        for group in range(groups)
+    ]
     return jnp.concatenate(columns, axis=1)
 
 
@@ -100,12 +103,8 @@
             left_ref[to, half * own : (half + 1) * own, :] = piece
 
 
-def square_part(own, halves, packed_ref, left_ref, out_ref, right_ref, left, arrived):
-    load = pltpu.make_async_copy(left_ref, left, arrived)
-    load.start()
-    right_ref[...] = panel(packed_ref, right_ref.shape[1] // BLK)
-    load.wait()
-    product = contract(right_ref[...], left[...])
+def square_part(own, halves, right_ref, left_ref, out_ref):
+    product = contract(panel(right_ref, right_ref.shape[1] // own), left_ref[...])
     rows = product.shape[0] // halves
     for rep in range(out_ref.shape[0]):
         for half in range(halves):
@@ -144,7 +143,7 @@
         placed[pl.ds(pl.multiple_of(half * rows + start, own), own), :] = (
             3.0 * square_ref[half * own : (half + 1) * own, :]
         )
-    product = contract(panel(low_ref, rows // BLK), right_ref[...])
+    product = contract(panel(low_ref, rows // BLK), panel(right_ref, cols // BLK))
     for down in range(rows // BLK):
         for across in range(cols // BLK):
             at = slice(down * BLK, (down + 1) * BLK), slice(across * BLK, (across + 1) * BLK)
@@ -175,16 +174,11 @@
         ],
     )(rep, pltpu.with_memory_space_constraint(density, pltpu.HBM))
     left = lax.all_to_all(left_copies, "col", 0, 0).reshape(col_count * part, rows)
-    left = pltpu.with_memory_space_constraint(left, pltpu.HBM)
-    right = gather(right_coded, "row")
-    parts, right = call(
+    right = gather(right_coded, "row", cols // BLK)
+    parts = call(
         functools.partial(square_part, own, halves),
-        (
-            shape((reps, part, rows), jnp.float32),
-            shape((right.shape[0] * own, cols), jnp.bfloat16),
-        ),
-        [VMEM, HBM],
-        [pltpu.VMEM(left.shape, left.dtype), pltpu.SemaphoreType.DMA],
+        shape((reps, part, rows), jnp.float32),
+        [VMEM, VMEM],
     )(right, left)
     parts = lax.all_to_all(parts, "rep", 0, 0)
     square, low_coded, factor = call(
@@ -196,7 +190,7 @@
         ),
         [SMEM, SMEM, SMEM, VMEM],
     )(rep, keep_square, keep_cube, parts)
-    low = gather(low_coded, "col")
+    low = gather(low_coded, "col", rows // BLK)
     total = call(
         functools.partial(cube_part, own, halves),
         shape((reps, own + HEAD, cols), jnp.float32),

time: 111 us -> 110 us (level)
  Pallas kernels: 7.36 us -> 6.01 us
    pallas_call x1, Pallas kernels: 2.7 us -> 1.41 us  [local(): call(functools.partial(square_part, own, halves), shape((reps, part, rows...]
  transfers between devices with their start and end apart: 1 -> 1, of which waited for: 0 -> 0; matrix products, arithmetic and copies ran while one was open for 0% -> 1% of each run, Pallas kernels for 0% -> 0%
where the time goes in v6:
time: 110 us
  blocking collectives  91.7 us (83%)
  starting transfers between devices  10.4 us (9%)
  Pallas kernels  6.01 us (5%)
  other arithmetic  1.83 us (2%)
    all_gather x2, blocking collectives, gather(): whole = lax.all_gather(packed.astype(jnp.float16), axis)  64.2 us
    all_to_all x1, blocking collectives, local(): parts = lax.all_to_all(parts, 'rep', 0, 0)  14.4 us
    all_to_all x1, blocking collectives, local(): lax.all_to_all(total.astype(jnp.float16), 'rep', 0, 0)  13 us
    all_to_all x1, starting transfers between devices, local(): lax.all_to_all(left_copies, 'col', 0, 0).reshape(col_count * part, rows)  10.4 us
    pallas_call x1, Pallas kernels, local(): call(functools.partial(prepare, own, halves), (shape((own * (cols // BLK)...  2.48 us
  transfers between devices with their start and end apart: 1, of which 0 were waited for; matrix products, arithmetic and copies ran while one was open for 1% of the time, Pallas kernels for 0%

profile of v6, /device:TPU:1, one launch (start us, length us, event | category | flops | bytes accessed | tf_op | source)
XLA Modules:
  0.0 110.0 jit_solution(3731429048108039987)
XLA Ops:
  0.0 2.5 %shard_map.37 = (bf16[584,128]{1,0:T(8,128)(2,1)S(1)}, bf16[8,192,384]{2,1,0:T(8,128)(2,1)}) custom-call(s32[1]{0:T(128)} %bitcast.rep_ref, bf16[384,768]{1,0:T(8,128)(2,1)} %tile_ref.1), custom_call_target="tpu_custom_call" | custom-call | tf_op jit(solution)/shard_map/pallas_call | solution.py:163
  2.5 10.4 %all-to-all-start = ((bf16[8,192,384]{2,1,0:T(8,128)(2,1)}), bf16[8,192,384]{2,1,0:T(8,128)(2,1)S(1)}, u32[]{:S(2)}, u32[]{:S(2)}) async-start(bf16[8,192,384]{2,1,0:T(8,128)(2,1)} %get-tuple-element.11), calls=%async_computation | async-start | bytes 2359296 | tf_op jit(solution)/shard_map/all_to_all | solution.py:176
  12.9 41.9 %all-gather.4 = f16[9344,128]{1,0:T(8,128)(2,1)S(1)} all-gather(f16[584,128]{1,0:T(8,128)(2,1)S(1)} %convert_element_type.33), channel_id=2, replica_groups=mesh['row'=16,'col'=8,'rep'=4] {'row'}, dimensions={0}, use_global_device_ids=true | all-gather | bytes 2541568 | tf_op jit(solution)/shard_map/all_gather | solution.py:67
  54.8 0.6 fusion.right_ref
  55.4 0.0 all-to-all-done
  55.4 1.4 %shard_map.38 = f32[4,192,384]{2,1,0:T(8,128)S(1)} custom-call(bf16[16,576,128]{2,1,0:T(8,128)(2,1)S(1)} %fusion.right_ref, bf16[1536,384]{1,0:T(8,128)(2,1)S(1)} %bitcast.15), custom_call_target="tpu_custom_call" | custom-call | tf_op jit(solution)/shard_map/pallas_call | solution.py:178
  56.8 0.0 copy-start
  56.8 0.0 copy-start.1
  56.8 14.4 %all_to_all.15.parts_ref = f32[4,192,384]{2,1,0:T(8,128)S(1)} all-to-all(f32[4,192,384]{2,1,0:T(8,128)S(1)} %shard_map.38), channel_id=1, replica_groups=mesh['row'=16,'col'=8,'rep'=4] {'rep'}, dimensions={0} | all-to-all | bytes 2359296 | tf_op jit(solution)/shard_map/all_to_all | solution.py:183
  71.2 0.0 copy-done
  71.2 0.0 copy-done.1
  71.3 0.8 shard_map.39
  72.1 22.3 %all-gather.5 = f16[4672,128]{1,0:T(8,128)(2,1)S(1)} all-gather(f16[584,128]{1,0:T(8,128)(2,1)S(1)} %convert_element_type.37), channel_id=3, replica_groups=mesh['row'=16,'col'=8,'rep'=4] {'col'}, dimensions={0}, use_global_device_ids=true | all-gather | bytes 1345536 | tf_op jit(solution)/shard_map/all_gather | solution.py:67
  94.4 0.2 fusion.1.low_ref
  94.7 1.4 %shard_map.40 = f32[4,104,768]{2,1,0:T(8,128)S(1)} custom-call(s32[1]{0:T(128)} %bitcast.rep_ref, f32[3,8,768]{2,1,0:T(8,128)S(1)} %get-tuple-element.12.factor_ref, bf16[8,576,128]{2,1,0:T(8,128)(2,1)S(1)} %fusion.1.low_ref, bf16[16,576,128]{2,1,0:T(8,128)(2,1)S(1)} %fusion.right_ref, f32[192,384]{1,0:T(8,128)S(1)} %get-tuple-element.14.square_ref), custom_call_target="tpu_custom_call" | custom-call | tf_op jit(solution)/shard_map/pallas_call | solution.py:194
  96.0 0.1 convert_element_type.41
  96.1 13.0 %all_to_all.16 = f16[4,104,768]{2,1,0:T(8,128)(2,1)S(1)} all-to-all(f16[4,104,768]{2,1,0:T(8,128)(2,1)S(1)} %convert_element_type.41), channel_id=1, replica_groups=mesh['row'=16,'col'=8,'rep'=4] {'rep'}, dimensions={0} | all-to-all | bytes 1277952 | tf_op jit(solution)/shard_map/all_to_all | solution.py:200
  109.1 0.8 multiply_reduce_fusion
  (6 shorter events, 0.1 us)
Async XLA Ops:
  2.5 52.9 %all-to-all-start = ((bf16[8,192,384]{2,1,0:T(8,128)(2,1)}), bf16[8,192,384]{2,1,0:T(8,128)(2,1)S(1)}, u32[]{:S(2)}, u32[]{:S(2)}) async-start(bf16[8,192,384]{2,1,0:T(8,128)(2,1)} %get-tuple-element.11), calls=%async_computation | async-start | bytes 2359296 | tf_op jit(solution)/shard_map/all_to_all | solution.py:176
  56.8 14.5 %copy-start = (s32[3,6]{1,0:T(4,128)S(1)}, s32[3,6]{1,0:T(4,128)}, u32[]{:S(2)}) copy-start(s32[3,6]{1,0:T(4,128)} %keep_ref.1) | copy-start | bytes 220
  56.8 14.4 %copy-start.1 = (s32[3,6]{1,0:T(4,128)S(1)}, s32[3,6]{1,0:T(4,128)}, u32[]{:S(2)}) copy-start(s32[3,6]{1,0:T(4,128)} %later_ref.1) | copy-start | bytes 220

commit v7 on v6

--- a/solution.py
+++ b/solution.py
@@ -80,6 +80,10 @@
         for group in range(groups)
     ]
     return jnp.concatenate(columns, axis=1)
+
+
+def window_start(start, rows, width):
+    return pl.multiple_of(jnp.minimum(lax.div(start, BLK) * BLK, rows - width), BLK)
 
 
 def prepare(own, halves, rep_ref, tile_ref, right_ref, left_ref, tile, turned, arrived):
@@ -96,15 +100,17 @@
         copy.wait()
     start = pl.multiple_of(rep_ref[0] * own, own)
     store_packed(right_ref, tile[pl.ds(start, own), :].astype(jnp.float32))
-    turned[...] = tile[...].T
+    width = turned.shape[0]
+    first = window_start(start, rows, width)
     for half in range(halves):
-        piece = turned[pl.ds(pl.multiple_of(half * rows + start, own), own), :]
+        turned[...] = tile[:, pl.ds(pl.multiple_of(half * rows + first, BLK), width)].T
+        piece = turned[pl.ds(pl.multiple_of(start - first, 16), own), :]
         for to in range(left_ref.shape[0]):
             left_ref[to, half * own : (half + 1) * own, :] = piece
 
 
 def square_part(own, halves, right_ref, left_ref, out_ref):
-    product = contract(panel(right_ref, right_ref.shape[1] // own), left_ref[...])
+    product = contract(left_ref[...], panel(right_ref, right_ref.shape[1] // own)).T
     rows = product.shape[0] // halves
     for rep in range(out_ref.shape[0]):
         for half in range(halves):
@@ -137,17 +143,21 @@
 
 def cube_part(own, halves, rep_ref, factor_ref, low_ref, right_ref, square_ref, out_ref, placed, total):
     rows, cols = total.shape
+    width = placed.shape[0]
     start = pl.multiple_of(rep_ref[0] * own, own)
-    placed[...] = jnp.zeros_like(placed)
-    for half in range(halves):
-        placed[pl.ds(pl.multiple_of(half * rows + start, own), own), :] = (
-            3.0 * square_ref[half * own : (half + 1) * own, :]
-        )
+    first = window_start(start, rows, width)
     product = contract(panel(low_ref, rows // BLK), panel(right_ref, cols // BLK))
     for down in range(rows // BLK):
         for across in range(cols // BLK):
             at = slice(down * BLK, (down + 1) * BLK), slice(across * BLK, (across + 1) * BLK)
-            total[at] = placed[at[1], at[0]].T + factor_ref[down, :1, at[1]] * product[at]
+            total[at] = factor_ref[down, :1, at[1]] * product[at]
+    placed[...] = jnp.zeros_like(placed)
+    for half in range(halves):
+        placed[pl.ds(pl.multiple_of(start - first, 8), own), :] = (
+            3.0 * square_ref[half * own : (half + 1) * own, :]
+        )
+        columns = pl.ds(pl.multiple_of(half * rows + first, BLK), width)
+        total[:, columns] = placed[...].T + total[:, columns]
     for rep in range(out_ref.shape[0]):
         store_coded(out_ref.at[rep], total[rep * own : (rep + 1) * own, :])
 
@@ -159,6 +169,7 @@
     rep = lax.axis_index("rep").astype(jnp.int32).reshape(1)
     shape = jax.ShapeDtypeStruct
     part = halves * own
+    width = -(-own // BLK) * BLK + BLK
 
     right_coded, left_copies = call(
         functools.partial(prepare, own, halves),
@@ -169,7 +180,7 @@
         [SMEM, HBM],
         [
             pltpu.VMEM((rows, cols), jnp.bfloat16),
-            pltpu.VMEM((cols, rows), jnp.bfloat16),
+            pltpu.VMEM((width, rows), jnp.bfloat16),
             pltpu.SemaphoreType.DMA((reps,)),
         ],
     )(rep, pltpu.with_memory_space_constraint(density, pltpu.HBM))
@@ -195,7 +206,7 @@
         functools.partial(cube_part, own, halves),
         shape((reps, own + HEAD, cols), jnp.float32),
         [SMEM, VMEM, VMEM, VMEM, VMEM],
-        [pltpu.VMEM((cols, rows), jnp.float32), pltpu.VMEM((rows, cols), jnp.float32)],
+        [pltpu.VMEM((width, rows), jnp.float32), pltpu.VMEM((rows, cols), jnp.float32)],
     )(rep, factor, low, right, square)
     return jnp.sum(decode(lax.all_to_all(total.astype(jnp.float16), "rep", 0, 0)), axis=0)
 

time: 110 us -> 110 us (level)
  no operation moved by 1% of the time
where the time goes in v7:
time: 110 us
  blocking collectives  91.7 us (83%)
  starting transfers between devices  10.4 us (9%)
  Pallas kernels  6.04 us (5%)
  other arithmetic  1.83 us (2%)
    all_gather x2, blocking collectives, gather(): whole = lax.all_gather(packed.astype(jnp.float16), axis)  64.2 us
    all_to_all x1, blocking collectives, local(): parts = lax.all_to_all(parts, 'rep', 0, 0)  14.4 us
    all_to_all x1, blocking collectives, local(): lax.all_to_all(total.astype(jnp.float16), 'rep', 0, 0)  13 us
    all_to_all x1, starting transfers between devices, local(): lax.all_to_all(left_copies, 'col', 0, 0).reshape(col_count * part, rows)  10.4 us
    pallas_call x1, Pallas kernels, local(): call(functools.partial(prepare, own, halves), (shape((own * (cols // BLK)...  2.42 us
  transfers between devices with their start and end apart: 1, of which 0 were waited for; matrix products, arithmetic and copies ran while one was open for 1% of the time, Pallas kernels for 0%

profile of v7, /device:TPU:1, one launch (start us, length us, event | category | flops | bytes accessed | tf_op | source)
XLA Modules:
  0.0 110.0 jit_solution(4758594495123516459)
XLA Ops:
  0.0 2.4 %shard_map.37 = (bf16[584,128]{1,0:T(8,128)(2,1)S(1)}, bf16[8,192,384]{2,1,0:T(8,128)(2,1)}) custom-call(s32[1]{0:T(128)} %bitcast.rep_ref, bf16[384,768]{1,0:T(8,128)(2,1)} %tile_ref.1), custom_call_target="tpu_custom_call" | custom-call | tf_op jit(solution)/shard_map/pallas_call | solution.py:174
  2.4 10.4 %all-to-all-start = ((bf16[8,192,384]{2,1,0:T(8,128)(2,1)}), bf16[8,192,384]{2,1,0:T(8,128)(2,1)S(1)}, u32[]{:S(2)}, u32[]{:S(2)}) async-start(bf16[8,192,384]{2,1,0:T(8,128)(2,1)} %get-tuple-element.11), calls=%async_computation | async-start | bytes 2359296 | tf_op jit(solution)/shard_map/all_to_all | solution.py:187
  12.8 41.9 %all-gather.4 = f16[9344,128]{1,0:T(8,128)(2,1)S(1)} all-gather(f16[584,128]{1,0:T(8,128)(2,1)S(1)} %convert_element_type.33), channel_id=2, replica_groups=mesh['row'=16,'col'=8,'rep'=4] {'row'}, dimensions={0}, use_global_device_ids=true | all-gather | bytes 2541568 | tf_op jit(solution)/shard_map/all_gather | solution.py:67
  54.7 0.6 fusion.right_ref
  55.3 0.0 all-to-all-done
  55.3 1.3 %shard_map.38 = f32[4,192,384]{2,1,0:T(8,128)S(1)} custom-call(bf16[16,576,128]{2,1,0:T(8,128)(2,1)S(1)} %fusion.right_ref, bf16[1536,384]{1,0:T(8,128)(2,1)S(1)} %bitcast.15), custom_call_target="tpu_custom_call" | custom-call | tf_op jit(solution)/shard_map/pallas_call | solution.py:189
  56.6 0.0 copy-start
  56.6 0.0 copy-start.1
  56.6 14.4 %all_to_all.15.parts_ref = f32[4,192,384]{2,1,0:T(8,128)S(1)} all-to-all(f32[4,192,384]{2,1,0:T(8,128)S(1)} %shard_map.38), channel_id=1, replica_groups=mesh['row'=16,'col'=8,'rep'=4] {'rep'}, dimensions={0} | all-to-all | bytes 2359296 | tf_op jit(solution)/shard_map/all_to_all | solution.py:194
  71.1 0.0 copy-done
  71.1 0.0 copy-done.1
  71.1 0.8 shard_map.39
  71.9 22.3 %all-gather.5 = f16[4672,128]{1,0:T(8,128)(2,1)S(1)} all-gather(f16[584,128]{1,0:T(8,128)(2,1)S(1)} %convert_element_type.37), channel_id=3, replica_groups=mesh['row'=16,'col'=8,'rep'=4] {'col'}, dimensions={0}, use_global_device_ids=true | all-gather | bytes 1345536 | tf_op jit(solution)/shard_map/all_gather | solution.py:67
  94.2 0.2 fusion.1.low_ref
  94.5 1.6 %shard_map.40 = f32[4,104,768]{2,1,0:T(8,128)S(1)} custom-call(s32[1]{0:T(128)} %bitcast.rep_ref, f32[3,8,768]{2,1,0:T(8,128)S(1)} %get-tuple-element.12.factor_ref, bf16[8,576,128]{2,1,0:T(8,128)(2,1)S(1)} %fusion.1.low_ref, bf16[16,576,128]{2,1,0:T(8,128)(2,1)S(1)} %fusion.right_ref, f32[192,384]{1,0:T(8,128)S(1)} %get-tuple-element.14.square_ref), custom_call_target="tpu_custom_call" | custom-call | tf_op jit(solution)/shard_map/pallas_call | solution.py:205
  96.0 0.1 convert_element_type.41
  96.1 13.0 %all_to_all.16 = f16[4,104,768]{2,1,0:T(8,128)(2,1)S(1)} all-to-all(f16[4,104,768]{2,1,0:T(8,128)(2,1)S(1)} %convert_element_type.41), channel_id=1, replica_groups=mesh['row'=16,'col'=8,'rep'=4] {'rep'}, dimensions={0} | all-to-all | bytes 1277952 | tf_op jit(solution)/shard_map/all_to_all | solution.py:211
  109.2 0.8 multiply_reduce_fusion
  (6 shorter events, 0.1 us)
Async XLA Ops:
  2.4 52.9 %all-to-all-start = ((bf16[8,192,384]{2,1,0:T(8,128)(2,1)}), bf16[8,192,384]{2,1,0:T(8,128)(2,1)S(1)}, u32[]{:S(2)}, u32[]{:S(2)}) async-start(bf16[8,192,384]{2,1,0:T(8,128)(2,1)} %get-tuple-element.11), calls=%async_computation | async-start | bytes 2359296 | tf_op jit(solution)/shard_map/all_to_all | solution.py:187
  56.6 14.5 %copy-start = (s32[3,6]{1,0:T(4,128)S(1)}, s32[3,6]{1,0:T(4,128)}, u32[]{:S(2)}) copy-start(s32[3,6]{1,0:T(4,128)} %keep_ref.1) | copy-start | bytes 220
  56.6 14.4 %copy-start.1 = (s32[3,6]{1,0:T(4,128)S(1)}, s32[3,6]{1,0:T(4,128)}, u32[]{:S(2)}) copy-start(s32[3,6]{1,0:T(4,128)} %later_ref.1) | copy-start | bytes 220

commit v8 on v6

--- a/solution.py
+++ b/solution.py
@@ -80,6 +80,10 @@
         for group in range(groups)
     ]
     return jnp.concatenate(columns, axis=1)
+
+
+def window_start(start, rows, width):
+    return pl.multiple_of(jnp.minimum(lax.div(start, BLK) * BLK, rows - width), BLK)
 
 
 def prepare(own, halves, rep_ref, tile_ref, right_ref, left_ref, tile, turned, arrived):
@@ -96,15 +100,17 @@
         copy.wait()
     start = pl.multiple_of(rep_ref[0] * own, own)
     store_packed(right_ref, tile[pl.ds(start, own), :].astype(jnp.float32))
-    turned[...] = tile[...].T
+    width = turned.shape[0]
+    first = window_start(start, rows, width)
     for half in range(halves):
-        piece = turned[pl.ds(pl.multiple_of(half * rows + start, own), own), :]
+        turned[...] = tile[:, pl.ds(pl.multiple_of(half * rows + first, BLK), width)].T
+        piece = turned[pl.ds(pl.multiple_of(start - first, 16), own), :]
         for to in range(left_ref.shape[0]):
             left_ref[to, half * own : (half + 1) * own, :] = piece
 
 
 def square_part(own, halves, right_ref, left_ref, out_ref):
-    product = contract(panel(right_ref, right_ref.shape[1] // own), left_ref[...])
+    product = contract(left_ref[...], panel(right_ref, right_ref.shape[1] // own)).T
     rows = product.shape[0] // halves
     for rep in range(out_ref.shape[0]):
         for half in range(halves):
@@ -159,6 +165,7 @@
     rep = lax.axis_index("rep").astype(jnp.int32).reshape(1)
     shape = jax.ShapeDtypeStruct
     part = halves * own
+    width = -(-own // BLK) * BLK + BLK
 
     right_coded, left_copies = call(
         functools.partial(prepare, own, halves),
@@ -169,7 +176,7 @@
         [SMEM, HBM],
         [
             pltpu.VMEM((rows, cols), jnp.bfloat16),
-            pltpu.VMEM((cols, rows), jnp.bfloat16),
+            pltpu.VMEM((width, rows), jnp.bfloat16),
             pltpu.SemaphoreType.DMA((reps,)),
         ],
     )(rep, pltpu.with_memory_space_constraint(density, pltpu.HBM))

time: 110 us -> 110 us (level)
  no operation moved by 1% of the time
where the time goes in v8:
time: 110 us
  blocking collectives  91.7 us (83%)
  starting transfers between devices  10.4 us (9%)
  Pallas kernels  5.84 us (5%)
  other arithmetic  1.83 us (2%)
    all_gather x2, blocking collectives, gather(): whole = lax.all_gather(packed.astype(jnp.float16), axis)  64.2 us
    all_to_all x1, blocking collectives, local(): parts = lax.all_to_all(parts, 'rep', 0, 0)  14.4 us
    all_to_all x1, blocking collectives, local(): lax.all_to_all(total.astype(jnp.float16), 'rep', 0, 0)  13 us
    all_to_all x1, starting transfers between devices, local(): lax.all_to_all(left_copies, 'col', 0, 0).reshape(col_count * part, rows)  10.4 us
    pallas_call x1, Pallas kernels, local(): call(functools.partial(prepare, own, halves), (shape((own * (cols // BLK)...  2.42 us
  transfers between devices with their start and end apart: 1, of which 0 were waited for; matrix products, arithmetic and copies ran while one was open for 1% of the time, Pallas kernels for 0%

profile of v8, /device:TPU:1, one launch (start us, length us, event | category | flops | bytes accessed | tf_op | source)
XLA Modules:
  0.0 109.8 jit_solution(9692233519880381061)
XLA Ops:
  0.0 2.4 %shard_map.37 = (bf16[584,128]{1,0:T(8,128)(2,1)S(1)}, bf16[8,192,384]{2,1,0:T(8,128)(2,1)}) custom-call(s32[1]{0:T(128)} %bitcast.rep_ref, bf16[384,768]{1,0:T(8,128)(2,1)} %tile_ref.1), custom_call_target="tpu_custom_call" | custom-call | tf_op jit(solution)/shard_map/pallas_call | solution.py:170
  2.4 10.4 %all-to-all-start = ((bf16[8,192,384]{2,1,0:T(8,128)(2,1)}), bf16[8,192,384]{2,1,0:T(8,128)(2,1)S(1)}, u32[]{:S(2)}, u32[]{:S(2)}) async-start(bf16[8,192,384]{2,1,0:T(8,128)(2,1)} %get-tuple-element.11), calls=%async_computation | async-start | bytes 2359296 | tf_op jit(solution)/shard_map/all_to_all | solution.py:183
  12.8 41.9 %all-gather.4 = f16[9344,128]{1,0:T(8,128)(2,1)S(1)} all-gather(f16[584,128]{1,0:T(8,128)(2,1)S(1)} %convert_element_type.33), channel_id=2, replica_groups=mesh['row'=16,'col'=8,'rep'=4] {'row'}, dimensions={0}, use_global_device_ids=true | all-gather | bytes 2541568 | tf_op jit(solution)/shard_map/all_gather | solution.py:67
  54.7 0.6 fusion.right_ref
  55.3 0.0 all-to-all-done
  55.3 1.3 %shard_map.38 = f32[4,192,384]{2,1,0:T(8,128)S(1)} custom-call(bf16[16,576,128]{2,1,0:T(8,128)(2,1)S(1)} %fusion.right_ref, bf16[1536,384]{1,0:T(8,128)(2,1)S(1)} %bitcast.15), custom_call_target="tpu_custom_call" | custom-call | tf_op jit(solution)/shard_map/pallas_call | solution.py:185
  56.6 0.0 copy-start
  56.6 0.0 copy-start.1
  56.6 14.4 %all_to_all.15.parts_ref = f32[4,192,384]{2,1,0:T(8,128)S(1)} all-to-all(f32[4,192,384]{2,1,0:T(8,128)S(1)} %shard_map.38), channel_id=1, replica_groups=mesh['row'=16,'col'=8,'rep'=4] {'rep'}, dimensions={0} | all-to-all | bytes 2359296 | tf_op jit(solution)/shard_map/all_to_all | solution.py:190
  71.1 0.0 copy-done
  71.1 0.0 copy-done.1
  71.1 0.8 shard_map.39
  71.9 22.3 %all-gather.5 = f16[4672,128]{1,0:T(8,128)(2,1)S(1)} all-gather(f16[584,128]{1,0:T(8,128)(2,1)S(1)} %convert_element_type.37), channel_id=3, replica_groups=mesh['row'=16,'col'=8,'rep'=4] {'col'}, dimensions={0}, use_global_device_ids=true | all-gather | bytes 1345536 | tf_op jit(solution)/shard_map/all_gather | solution.py:67
  94.2 0.2 fusion.1.low_ref
  94.5 1.4 %shard_map.40 = f32[4,104,768]{2,1,0:T(8,128)S(1)} custom-call(s32[1]{0:T(128)} %bitcast.rep_ref, f32[3,8,768]{2,1,0:T(8,128)S(1)} %get-tuple-element.12.factor_ref, bf16[8,576,128]{2,1,0:T(8,128)(2,1)S(1)} %fusion.1.low_ref, bf16[16,576,128]{2,1,0:T(8,128)(2,1)S(1)} %fusion.right_ref, f32[192,384]{1,0:T(8,128)S(1)} %get-tuple-element.14.square_ref), custom_call_target="tpu_custom_call" | custom-call | tf_op jit(solution)/shard_map/pallas_call | solution.py:201
  95.8 0.1 convert_element_type.41
  95.9 13.0 %all_to_all.16 = f16[4,104,768]{2,1,0:T(8,128)(2,1)S(1)} all-to-all(f16[4,104,768]{2,1,0:T(8,128)(2,1)S(1)} %convert_element_type.41), channel_id=1, replica_groups=mesh['row'=16,'col'=8,'rep'=4] {'rep'}, dimensions={0} | all-to-all | bytes 1277952 | tf_op jit(solution)/shard_map/all_to_all | solution.py:207
  109.0 0.8 multiply_reduce_fusion
  (6 shorter events, 0.1 us)
Async XLA Ops:
  2.4 52.9 %all-to-all-start = ((bf16[8,192,384]{2,1,0:T(8,128)(2,1)}), bf16[8,192,384]{2,1,0:T(8,128)(2,1)S(1)}, u32[]{:S(2)}, u32[]{:S(2)}) async-start(bf16[8,192,384]{2,1,0:T(8,128)(2,1)} %get-tuple-element.11), calls=%async_computation | async-start | bytes 2359296 | tf_op jit(solution)/shard_map/all_to_all | solution.py:183
  56.6 14.5 %copy-start = (s32[3,6]{1,0:T(4,128)S(1)}, s32[3,6]{1,0:T(4,128)}, u32[]{:S(2)}) copy-start(s32[3,6]{1,0:T(4,128)} %keep_ref.1) | copy-start | bytes 220
  56.6 14.4 %copy-start.1 = (s32[3,6]{1,0:T(4,128)S(1)}, s32[3,6]{1,0:T(4,128)}, u32[]{:S(2)}) copy-start(s32[3,6]{1,0:T(4,128)} %later_ref.1) | copy-start | bytes 220

commit v9 on v8

--- a/solution.py
+++ b/solution.py
@@ -58,9 +58,11 @@
 
 
 def decode(pieces):
-    height = pieces.shape[1] - HEAD
-    scale = jnp.exp2(pieces[:, height : height + 1, :].astype(jnp.float32))
-    return pieces[:, :height, :].astype(jnp.float32) * (1.0 / TOP) * scale
+    count, height, width = pieces.shape
+    height -= HEAD
+    scale = jnp.exp2(pieces[:, height:, :].astype(jnp.float32)) * (1.0 / TOP)
+    scale = jnp.broadcast_to(scale[:, None], (count, height // HEAD, HEAD, width))
+    return pieces[:, :height, :].astype(jnp.float32) * scale.reshape(count, height, width)
 
 
 def gather(packed, axis, groups):

time: 110 us -> 110 us (level)
  no operation moved by 1% of the time
where the time goes in v9:
time: 110 us
  blocking collectives  91.7 us (83%)
  starting transfers between devices  10.4 us (9%)
  Pallas kernels  5.84 us (5%)
  other arithmetic  1.83 us (2%)
    all_gather x2, blocking collectives, gather(): whole = lax.all_gather(packed.astype(jnp.float16), axis)  64.2 us
    all_to_all x1, blocking collectives, local(): parts = lax.all_to_all(parts, 'rep', 0, 0)  14.4 us
    all_to_all x1, blocking collectives, local(): lax.all_to_all(total.astype(jnp.float16), 'rep', 0, 0)  13 us
    all_to_all x1, starting transfers between devices, local(): lax.all_to_all(left_copies, 'col', 0, 0).reshape(col_count * part, rows)  10.4 us
    pallas_call x1, Pallas kernels, local(): call(functools.partial(prepare, own, halves), (shape((own * (cols // BLK)...  2.42 us
  transfers between devices with their start and end apart: 1, of which 0 were waited for; matrix products, arithmetic and copies ran while one was open for 1% of the time, Pallas kernels for 0%

profile of v9, /device:TPU:1, one launch (start us, length us, event | category | flops | bytes accessed | tf_op | source)
XLA Modules:
  0.0 109.8 jit_solution(8901811773639041037)
XLA Ops:
  0.0 2.4 %shard_map.37 = (bf16[584,128]{1,0:T(8,128)(2,1)S(1)}, bf16[8,192,384]{2,1,0:T(8,128)(2,1)}) custom-call(s32[1]{0:T(128)} %bitcast.rep_ref, bf16[384,768]{1,0:T(8,128)(2,1)} %tile_ref.1), custom_call_target="tpu_custom_call" | custom-call | tf_op jit(solution)/shard_map/pallas_call | solution.py:172
  2.4 10.4 %all-to-all-start = ((bf16[8,192,384]{2,1,0:T(8,128)(2,1)}), bf16[8,192,384]{2,1,0:T(8,128)(2,1)S(1)}, u32[]{:S(2)}, u32[]{:S(2)}) async-start(bf16[8,192,384]{2,1,0:T(8,128)(2,1)} %get-tuple-element.11), calls=%async_computation | async-start | bytes 2359296 | tf_op jit(solution)/shard_map/all_to_all | solution.py:185
  12.8 41.9 %all-gather.4 = f16[9344,128]{1,0:T(8,128)(2,1)S(1)} all-gather(f16[584,128]{1,0:T(8,128)(2,1)S(1)} %convert_element_type.33), channel_id=2, replica_groups=mesh['row'=16,'col'=8,'rep'=4] {'row'}, dimensions={0}, use_global_device_ids=true | all-gather | bytes 2541568 | tf_op jit(solution)/shard_map/all_gather | solution.py:69
  54.7 0.6 fusion.right_ref
  55.3 0.0 all-to-all-done
  55.3 1.3 %shard_map.38 = f32[4,192,384]{2,1,0:T(8,128)S(1)} custom-call(bf16[16,576,128]{2,1,0:T(8,128)(2,1)S(1)} %fusion.right_ref, bf16[1536,384]{1,0:T(8,128)(2,1)S(1)} %bitcast.16), custom_call_target="tpu_custom_call" | custom-call | tf_op jit(solution)/shard_map/pallas_call | solution.py:187
  56.6 0.0 copy-start
  56.6 0.0 copy-start.1
  56.6 14.4 %all_to_all.15.parts_ref = f32[4,192,384]{2,1,0:T(8,128)S(1)} all-to-all(f32[4,192,384]{2,1,0:T(8,128)S(1)} %shard_map.38), channel_id=1, replica_groups=mesh['row'=16,'col'=8,'rep'=4] {'rep'}, dimensions={0} | all-to-all | bytes 2359296 | tf_op jit(solution)/shard_map/all_to_all | solution.py:192
  71.1 0.0 copy-done
  71.1 0.0 copy-done.1
  71.1 0.8 shard_map.39
  71.9 22.3 %all-gather.5 = f16[4672,128]{1,0:T(8,128)(2,1)S(1)} all-gather(f16[584,128]{1,0:T(8,128)(2,1)S(1)} %convert_element_type.37), channel_id=3, replica_groups=mesh['row'=16,'col'=8,'rep'=4] {'col'}, dimensions={0}, use_global_device_ids=true | all-gather | bytes 1345536 | tf_op jit(solution)/shard_map/all_gather | solution.py:69
  94.2 0.2 fusion.1.low_ref
  94.5 1.4 %shard_map.40 = f32[4,104,768]{2,1,0:T(8,128)S(1)} custom-call(s32[1]{0:T(128)} %bitcast.rep_ref, f32[3,8,768]{2,1,0:T(8,128)S(1)} %get-tuple-element.12.factor_ref, bf16[8,576,128]{2,1,0:T(8,128)(2,1)S(1)} %fusion.1.low_ref, bf16[16,576,128]{2,1,0:T(8,128)(2,1)S(1)} %fusion.right_ref, f32[192,384]{1,0:T(8,128)S(1)} %get-tuple-element.14.square_ref), custom_call_target="tpu_custom_call" | custom-call | tf_op jit(solution)/shard_map/pallas_call | solution.py:203
  95.8 0.1 convert_element_type.41
  95.9 13.0 %all_to_all.16 = f16[4,104,768]{2,1,0:T(8,128)(2,1)S(1)} all-to-all(f16[4,104,768]{2,1,0:T(8,128)(2,1)S(1)} %convert_element_type.41), channel_id=1, replica_groups=mesh['row'=16,'col'=8,'rep'=4] {'rep'}, dimensions={0} | all-to-all | bytes 1277952 | tf_op jit(solution)/shard_map/all_to_all | solution.py:209
  108.9 0.8 fusion.2
  (5 shorter events, 0.1 us)
Async XLA Ops:
  2.4 52.9 %all-to-all-start = ((bf16[8,192,384]{2,1,0:T(8,128)(2,1)}), bf16[8,192,384]{2,1,0:T(8,128)(2,1)S(1)}, u32[]{:S(2)}, u32[]{:S(2)}) async-start(bf16[8,192,384]{2,1,0:T(8,128)(2,1)} %get-tuple-element.11), calls=%async_computation | async-start | bytes 2359296 | tf_op jit(solution)/shard_map/all_to_all | solution.py:185
  56.6 14.5 %copy-start = (s32[3,6]{1,0:T(4,128)S(1)}, s32[3,6]{1,0:T(4,128)}, u32[]{:S(2)}) copy-start(s32[3,6]{1,0:T(4,128)} %keep_ref.1) | copy-start | bytes 220
  56.6 14.4 %copy-start.1 = (s32[3,6]{1,0:T(4,128)S(1)}, s32[3,6]{1,0:T(4,128)}, u32[]{:S(2)}) copy-start(s32[3,6]{1,0:T(4,128)} %later_ref.1) | copy-start | bytes 220

commit v10 on v9

--- a/solution.py
+++ b/solution.py
@@ -92,23 +92,28 @@
     rows = tile_ref.shape[0]
     copies = [
         pltpu.make_async_copy(
-            tile_ref.at[pl.ds(part * own, own), :], tile.at[pl.ds(part * own, own), :], arrived.at[part]
+            tile_ref.at[part * BLK : (part + 1) * BLK, :],
+            tile.at[part * BLK : (part + 1) * BLK, :],
+            arrived.at[part],
         )
-        for part in range(rows // own)
+        for part in range(rows // BLK)
     ]
     for copy in copies:
         copy.start()
-    for copy in copies:
+    start = pl.multiple_of(rep_ref[0] * own, own)
+    width = turned.shape[1]
+    first = window_start(start, rows, width)
+    for part, copy in enumerate(copies):
         copy.wait()
-    start = pl.multiple_of(rep_ref[0] * own, own)
-    store_packed(right_ref, tile[pl.ds(start, own), :].astype(jnp.float32))
-    width = turned.shape[0]
-    first = window_start(start, rows, width)
+        at = slice(part * BLK, (part + 1) * BLK)
+        for half in range(halves):
+            columns = pl.ds(pl.multiple_of(half * rows + first, BLK), width)
+            turned[half, :, at] = tile[at, columns].T
     for half in range(halves):
-        turned[...] = tile[:, pl.ds(pl.multiple_of(half * rows + first, BLK), width)].T
-        piece = turned[pl.ds(pl.multiple_of(start - first, 16), own), :]
+        piece = turned[half, pl.ds(pl.multiple_of(start - first, 16), own), :]
         for to in range(left_ref.shape[0]):
             left_ref[to, half * own : (half + 1) * own, :] = piece
+    store_packed(right_ref, tile[pl.ds(start, own), :].astype(jnp.float32))
 
 
 def square_part(own, halves, right_ref, left_ref, out_ref):
@@ -178,8 +183,8 @@
         [SMEM, HBM],
         [
             pltpu.VMEM((rows, cols), jnp.bfloat16),
-            pltpu.VMEM((width, rows), jnp.bfloat16),
-            pltpu.SemaphoreType.DMA((reps,)),
+            pltpu.VMEM((halves, width, rows), jnp.bfloat16),
+            pltpu.SemaphoreType.DMA((rows // BLK,)),
         ],
     )(rep, pltpu.with_memory_space_constraint(density, pltpu.HBM))
     left = lax.all_to_all(left_copies, "col", 0, 0).reshape(col_count * part, rows)

time: 110 us -> 110 us (level)
  no operation moved by 1% of the time
where the time goes in v10:
time: 110 us
  blocking collectives  91.7 us (83%)
  starting transfers between devices  10.4 us (9%)
  Pallas kernels  5.75 us (5%)
  other arithmetic  1.83 us (2%)
    all_gather x2, blocking collectives, gather(): whole = lax.all_gather(packed.astype(jnp.float16), axis)  64.2 us
    all_to_all x1, blocking collectives, local(): parts = lax.all_to_all(parts, 'rep', 0, 0)  14.4 us
    all_to_all x1, blocking collectives, local(): lax.all_to_all(total.astype(jnp.float16), 'rep', 0, 0)  13 us
    all_to_all x1, starting transfers between devices, local(): lax.all_to_all(left_copies, 'col', 0, 0).reshape(col_count * part, rows)  10.4 us
    pallas_call x1, Pallas kernels, local(): call(functools.partial(prepare, own, halves), (shape((own * (cols // BLK)...  2.35 us
  transfers between devices with their start and end apart: 1, of which 0 were waited for; matrix products, arithmetic and copies ran while one was open for 1% of the time, Pallas kernels for 0%

profile of v10, /device:TPU:1, one launch (start us, length us, event | category | flops | bytes accessed | tf_op | source)
XLA Modules:
  0.0 109.7 jit_solution(1859131640379606498)
XLA Ops:
  0.0 2.3 %shard_map.37 = (bf16[584,128]{1,0:T(8,128)(2,1)S(1)}, bf16[8,192,384]{2,1,0:T(8,128)(2,1)}) custom-call(s32[1]{0:T(128)} %bitcast.rep_ref, bf16[384,768]{1,0:T(8,128)(2,1)} %tile_ref.1), custom_call_target="tpu_custom_call" | custom-call | tf_op jit(solution)/shard_map/pallas_call | solution.py:177
  2.4 10.4 %all-to-all-start = ((bf16[8,192,384]{2,1,0:T(8,128)(2,1)}), bf16[8,192,384]{2,1,0:T(8,128)(2,1)S(1)}, u32[]{:S(2)}, u32[]{:S(2)}) async-start(bf16[8,192,384]{2,1,0:T(8,128)(2,1)} %get-tuple-element.11), calls=%async_computation | async-start | bytes 2359296 | tf_op jit(solution)/shard_map/all_to_all | solution.py:190
  12.7 41.9 %all-gather.4 = f16[9344,128]{1,0:T(8,128)(2,1)S(1)} all-gather(f16[584,128]{1,0:T(8,128)(2,1)S(1)} %convert_element_type.33), channel_id=2, replica_groups=mesh['row'=16,'col'=8,'rep'=4] {'row'}, dimensions={0}, use_global_device_ids=true | all-gather | bytes 2541568 | tf_op jit(solution)/shard_map/all_gather | solution.py:69
  54.7 0.6 fusion.right_ref
  55.2 0.0 all-to-all-done
  55.2 1.3 %shard_map.38 = f32[4,192,384]{2,1,0:T(8,128)S(1)} custom-call(bf16[16,576,128]{2,1,0:T(8,128)(2,1)S(1)} %fusion.right_ref, bf16[1536,384]{1,0:T(8,128)(2,1)S(1)} %bitcast.16), custom_call_target="tpu_custom_call" | custom-call | tf_op jit(solution)/shard_map/pallas_call | solution.py:192
  56.5 0.0 copy-start
  56.6 0.0 copy-start.1
  56.6 14.4 %all_to_all.15.parts_ref = f32[4,192,384]{2,1,0:T(8,128)S(1)} all-to-all(f32[4,192,384]{2,1,0:T(8,128)S(1)} %shard_map.38), channel_id=1, replica_groups=mesh['row'=16,'col'=8,'rep'=4] {'rep'}, dimensions={0} | all-to-all | bytes 2359296 | tf_op jit(solution)/shard_map/all_to_all | solution.py:197
  71.0 0.0 copy-done
  71.0 0.0 copy-done.1
  71.0 0.8 shard_map.39
  71.8 22.3 %all-gather.5 = f16[4672,128]{1,0:T(8,128)(2,1)S(1)} all-gather(f16[584,128]{1,0:T(8,128)(2,1)S(1)} %convert_element_type.37), channel_id=3, replica_groups=mesh['row'=16,'col'=8,'rep'=4] {'col'}, dimensions={0}, use_global_device_ids=true | all-gather | bytes 1345536 | tf_op jit(solution)/shard_map/all_gather | solution.py:69
  94.2 0.2 fusion.1.low_ref
  94.4 1.4 %shard_map.40 = f32[4,104,768]{2,1,0:T(8,128)S(1)} custom-call(s32[1]{0:T(128)} %bitcast.rep_ref, f32[3,8,768]{2,1,0:T(8,128)S(1)} %get-tuple-element.12.factor_ref, bf16[8,576,128]{2,1,0:T(8,128)(2,1)S(1)} %fusion.1.low_ref, bf16[16,576,128]{2,1,0:T(8,128)(2,1)S(1)} %fusion.right_ref, f32[192,384]{1,0:T(8,128)S(1)} %get-tuple-element.14.square_ref), custom_call_target="tpu_custom_call" | custom-call | tf_op jit(solution)/shard_map/pallas_call | solution.py:208
  95.8 0.1 convert_element_type.41
  95.8 13.0 %all_to_all.16 = f16[4,104,768]{2,1,0:T(8,128)(2,1)S(1)} all-to-all(f16[4,104,768]{2,1,0:T(8,128)(2,1)S(1)} %convert_element_type.41), channel_id=1, replica_groups=mesh['row'=16,'col'=8,'rep'=4] {'rep'}, dimensions={0} | all-to-all | bytes 1277952 | tf_op jit(solution)/shard_map/all_to_all | solution.py:214
  108.9 0.8 fusion.2
  (5 shorter events, 0.1 us)
Async XLA Ops:
  2.4 52.9 %all-to-all-start = ((bf16[8,192,384]{2,1,0:T(8,128)(2,1)}), bf16[8,192,384]{2,1,0:T(8,128)(2,1)S(1)}, u32[]{:S(2)}, u32[]{:S(2)}) async-start(bf16[8,192,384]{2,1,0:T(8,128)(2,1)} %get-tuple-element.11), calls=%async_computation | async-start | bytes 2359296 | tf_op jit(solution)/shard_map/all_to_all | solution.py:190
  56.5 14.5 %copy-start = (s32[3,6]{1,0:T(4,128)S(1)}, s32[3,6]{1,0:T(4,128)}, u32[]{:S(2)}) copy-start(s32[3,6]{1,0:T(4,128)} %keep_ref.1) | copy-start | bytes 220
  56.6 14.4 %copy-start.1 = (s32[3,6]{1,0:T(4,128)S(1)}, s32[3,6]{1,0:T(4,128)}, u32[]{:S(2)}) copy-start(s32[3,6]{1,0:T(4,128)} %later_ref.1) | copy-start | bytes 220
